TPU v7x, 32 devices: a whole 2x2x4 slice. The times are simulated.
32 devices in a mesh: dp: 8 (over z, y), head: 4 (over x, core).
Axes of the slice: x: 2, y: 2, z: 4, core: 2. Of those that a mesh axis runs over, the one named last changes fastest.
Arguments:
- block_input_rows: bfloat16 [32, 1024, 1024], P('dp', 'head'), may hold values from -6 to 6
- document_starts: int32 [32, 1024], P('dp'), may hold values from 0 to 1023, as said below
- counted_mask: int32 [32, 1024], P('dp', 'head'), may hold values from 0 to 1
- output_gradient: bfloat16 [32, 1024, 1024], P('dp', 'head'), may hold values from -6 to 6
- first_norm_gain: bfloat16 [1024], replicated, may hold values from 0.099609375 to 1.8984375
- first_norm_bias: bfloat16 [1024], replicated, may hold values from -4 to 4
- query_key_value_weight: bfloat16 [1024, 3072], replicated, may hold values from -0.1875 to 0.1875
- query_down_weight: bfloat16 [1024, 4], replicated, may hold values from -0.1875 to 0.1875
- query_up_weight: bfloat16 [4, 1024], replicated, may hold values from -0.75 to 0.75
- value_down_weight: bfloat16 [1024, 4], replicated, may hold values from -0.1875 to 0.1875
- value_up_weight: bfloat16 [4, 1024], replicated, may hold values from -0.75 to 0.75
- attention_out_weight: bfloat16 [1024, 1024], replicated, may hold values from -0.75 to 0.75
- second_norm_gain: bfloat16 [1024], replicated, may hold values from 0.099609375 to 1.8984375
- second_norm_bias: bfloat16 [1024], replicated, may hold values from -4 to 4
- feed_input_weight: bfloat16 [1024, 4096], replicated, may hold values from -0.1875 to 0.1875
- feed_input_bias: bfloat16 [4096], replicated, may hold values from -6 to 6
- feed_output_weight: bfloat16 [4096, 1024], replicated, may hold values from -0.09375 to 0.09375
Outputs:
- output: bfloat16 [32, 1024, 1024], P('dp', 'head')
- input_grad: bfloat16 [32, 1024, 1024], P('dp', 'head')
- grad_lora_aq: float32 [1024, 4], replicated
- grad_lora_bq: float32 [4, 1024], replicated
- grad_lora_av: float32 [1024, 4], replicated
- grad_lora_bv: float32 [4, 1024], replicated
- rms_values: float32 [2], replicated
Inputs may be any that keep to these rules, and one draw needn't show every extreme that they name: `document_starts`: within each slot a token's id is the position of the first token of its document, so ids never fall along the slot. In each aligned group of 4 slots one slot, drawn from the seed, is a single document; in every other slot the last token is a document of its own.
All inputs are finite; a program needn't handle non-finite values.
Results may differ from a plain program's by a relative error of at most 0.013.
Values may be sent and summed in bfloat16 or wider, within the bound.
A program may use at most 192 MiB of HBM per device.

v0:
```python
import functools

import jax
import jax.numpy as jnp
from jax import lax
from jax.experimental import pallas as pl
from jax.experimental.pallas import tpu as pltpu
from jax.sharding import PartitionSpec as P

H = 16


EPSILON = 1e-05
ADAPTER_SCALE = 8.0
NEGATIVE = -1e30


def as_sent(x):

    def short(part):
        return part.astype(jnp.bfloat16) if part.dtype == jnp.float32 else part

    return jax.tree.map(short, x)


def norm_rows(matrix, gain_vec, shift_vec):
    center = matrix - jnp.mean(matrix, axis=-1, keepdims=True)
    variance = jnp.mean(center * center, axis=-1, keepdims=True)
    return center * lax.rsqrt(variance + EPSILON) * gain_vec + shift_vec


def norm_back(matrix, gain_vec, shift_vec, incoming):
    pullback = jax.vjp(lambda element_item: norm_rows(element_item, gain_vec, shift_vec), matrix)[1]
    return pullback(incoming)[0]


def gelu_tanh(matrix):
    return jax.nn.gelu(matrix, approximate=True)


def plain_product(left, right):
    return jnp.dot(left, right, preferred_element_type=jnp.float32)


def last_product(left, right):
    return lax.dot_general(
        left, right, (((1,), (1,)), ((), ())), preferred_element_type=jnp.float32
    )


def first_product(left, right):
    return lax.dot_general(
        left, right, (((0,), (0,)), ((), ())), preferred_element_type=jnp.float32
    )


def masked_scores(query_block, key_slot, segments, row_start, row_end, score_scale):
    places = jnp.arange(row_end)
    allowed = (segments[row_start:row_end, None] == segments[None, :row_end]) & (
        places[None, :] <= places[row_start:row_end, None]
    )
    scores = (
        jnp.einsum(
            "qhd,khd->hqk", query_block, key_slot[:row_end], preferred_element_type=jnp.float32
        )
        * score_scale
    )
    return jnp.where(allowed[None], scores, NEGATIVE)


def attend_slot(query_slot, key_slot, value_slot, segments, block_rows, score_scale):
    length = query_slot.shape[0]
    outputs_list = []
    logsum_list = []
    for block_index in range(length // block_rows):
        row_start = block_index * block_rows
        row_end = row_start + block_rows
        scores = masked_scores(
            query_slot[row_start:row_end], key_slot, segments, row_start, row_end, score_scale
        )
        row_max = jnp.max(scores, axis=-1, keepdims=True)
        exponent = jnp.exp(scores - row_max)
        row_total = jnp.sum(exponent, axis=-1, keepdims=True)
        probability = (exponent / row_total).astype(jnp.bfloat16)
        context = jnp.einsum(
            "hqk,khd->qhd", probability, value_slot[:row_end], preferred_element_type=jnp.float32
        )
        outputs_list.append(context.astype(jnp.bfloat16))
        logsum_list.append((row_max + jnp.log(row_total))[..., 0])
    return (jnp.concatenate(outputs_list, 0), jnp.concatenate(logsum_list, 1))


def attend_back(
    query_slot, key_slot, value_slot, grad_slot, logsum, segments, block_rows, score_scale
):
    length = query_slot.shape[0]
    key_grad = jnp.zeros(key_slot.shape, jnp.float32)
    value_gradient = jnp.zeros(value_slot.shape, jnp.float32)
    query_parts = []
    for block_index in range(length // block_rows):
        row_start = block_index * block_rows
        row_end = row_start + block_rows
        query_block = query_slot[row_start:row_end]
        grad_block = grad_slot[row_start:row_end]
        scores = masked_scores(query_block, key_slot, segments, row_start, row_end, score_scale)
        probability = jnp.exp(scores - logsum[:, row_start:row_end, None])
        prob_grad = jnp.einsum(
            "qhd,khd->hqk", grad_block, value_slot[:row_end], preferred_element_type=jnp.float32
        )
        inner_sum = jnp.sum(probability * prob_grad, axis=-1, keepdims=True)
        score_grad = (probability * (prob_grad - inner_sum)).astype(jnp.bfloat16)
        query_parts.append(
            jnp.einsum(
                "hqk,khd->qhd", score_grad, key_slot[:row_end], preferred_element_type=jnp.float32
            )
            * score_scale
        )
        key_grad = key_grad.at[:row_end].add(
            jnp.einsum("hqk,qhd->khd", score_grad, query_block, preferred_element_type=jnp.float32)
            * score_scale
        )
        value_gradient = value_gradient.at[:row_end].add(
            jnp.einsum(
                "hqk,qhd->khd",
                probability.astype(jnp.bfloat16),
                grad_block,
                preferred_element_type=jnp.float32,
            )
        )
    query_gradient = jnp.concatenate(query_parts, 0)
    return (
        query_gradient.astype(jnp.bfloat16),
        key_grad.astype(jnp.bfloat16),
        value_gradient.astype(jnp.bfloat16),
    )


def shards(
    block_input_rows,
    document_starts,
    counted_mask,
    output_gradient,
    first_norm_gain,
    first_norm_bias,
    query_key_value_weight,
    query_down_weight,
    query_up_weight,
    value_down_weight,
    value_up_weight,
    attention_out_weight,
    second_norm_gain,
    second_norm_bias,
    feed_input_weight,
    feed_input_bias,
    feed_output_weight,
):
    slot_count, local_len, row_width = block_input_rows.shape
    groups = lax.axis_size("head")
    full_len = local_len * groups
    head_size = row_width // H
    heads_here = H // groups
    row_count = slot_count * local_len
    block_rows = min(512, full_len)
    score_scale = head_size ** (-0.5)
    gain_one = first_norm_gain.astype(jnp.float32)
    shift_one = first_norm_bias.astype(jnp.float32)
    gain_two = second_norm_gain.astype(jnp.float32)
    shift_two = second_norm_bias.astype(jnp.float32)
    fc_bias = feed_input_bias.astype(jnp.float32)
    local_shape = (slot_count, local_len, row_width)
    split_shape = (slot_count, full_len, heads_here, head_size)
    merged_shape = (slot_count, full_len, heads_here * head_size)
    flat_in = block_input_rows.reshape(row_count, row_width).astype(jnp.float32)
    normed_rows = norm_rows(flat_in, gain_one, shift_one).astype(jnp.bfloat16)
    query_low_rank = plain_product(normed_rows, query_down_weight).astype(jnp.bfloat16)
    value_low_rank = plain_product(normed_rows, value_down_weight).astype(jnp.bfloat16)
    projected_rows = plain_product(normed_rows, query_key_value_weight)
    query_rows = (
        projected_rows[:, :row_width]
        + ADAPTER_SCALE * plain_product(query_low_rank, query_up_weight)
    ).astype(jnp.bfloat16)
    key_rows = projected_rows[:, row_width : 2 * row_width].astype(jnp.bfloat16)
    value_matrix = (
        projected_rows[:, 2 * row_width :]
        + ADAPTER_SCALE * plain_product(value_low_rank, value_up_weight)
    ).astype(jnp.bfloat16)
    head_query, head_key, head_value = (
        lax.all_to_all(
            query_rows.reshape(local_shape), "head", split_axis=2, concat_axis=1, tiled=True
        ),
        lax.all_to_all(
            key_rows.reshape(local_shape), "head", split_axis=2, concat_axis=1, tiled=True
        ),
        lax.all_to_all(
            value_matrix.reshape(local_shape), "head", split_axis=2, concat_axis=1, tiled=True
        ),
    )
    head_query = head_query.reshape(split_shape)
    head_key = head_key.reshape(split_shape)
    head_value = head_value.reshape(split_shape)

    def slot_fn(packed):
        return attend_slot(packed[0], packed[1], packed[2], packed[3], block_rows, score_scale)

    context_heads, logsum = lax.map(slot_fn, (head_query, head_key, head_value, document_starts))
    context_local = lax.all_to_all(
        as_sent(context_heads.reshape(merged_shape)),
        "head",
        split_axis=1,
        concat_axis=2,
        tiled=True,
    )
    context_flat = context_local.reshape(row_count, row_width)
    branch = plain_product(context_flat, attention_out_weight)
    hidden_state = flat_in + branch
    normed_two = norm_rows(hidden_state, gain_two, shift_two).astype(jnp.bfloat16)
    before = plain_product(normed_two, feed_input_weight) + fc_bias
    activated = gelu_tanh(before).astype(jnp.bfloat16)
    feed_out = plain_product(activated, feed_output_weight)
    result = hidden_state + feed_out
    output = result.astype(jnp.bfloat16).reshape(block_input_rows.shape)
    valid_rows = counted_mask.reshape(row_count).astype(jnp.float32)[:, None]
    square_sums = jnp.stack(
        [
            jnp.sum(valid_rows * result * result),
            jnp.sum(valid_rows * (branch * branch + feed_out * feed_out)),
            jnp.sum(valid_rows),
        ]
    )
    grad_flat = output_gradient.reshape(row_count, row_width)
    act_grad = last_product(grad_flat, feed_output_weight)
    gelu_pull = jax.vjp(gelu_tanh, before)[1]
    before_grad = gelu_pull(act_grad)[0].astype(jnp.bfloat16)
    normed_two_grad = last_product(before_grad, feed_input_weight)
    hidden_grad = grad_flat.astype(jnp.float32) + norm_back(
        hidden_state, gain_two, shift_two, normed_two_grad
    )
    branch_grad = hidden_grad.astype(jnp.bfloat16)
    context_grad = last_product(branch_grad, attention_out_weight).astype(jnp.bfloat16)
    grad_heads = lax.all_to_all(
        context_grad.reshape(local_shape), "head", split_axis=2, concat_axis=1, tiled=True
    ).reshape(split_shape)

    def back_fn(packed):
        return attend_back(
            packed[0],
            packed[1],
            packed[2],
            packed[3],
            packed[4],
            packed[5],
            block_rows,
            score_scale,
        )

    query_gradient, key_grad, value_gradient = lax.map(
        back_fn, (head_query, head_key, head_value, grad_heads, logsum, document_starts)
    )
    query_gradient, key_grad, value_gradient = (
        lax.all_to_all(
            as_sent(query_gradient.reshape(merged_shape)),
            "head",
            split_axis=1,
            concat_axis=2,
            tiled=True,
        ),
        lax.all_to_all(
            as_sent(key_grad.reshape(merged_shape)), "head", split_axis=1, concat_axis=2, tiled=True
        ),
        lax.all_to_all(
            as_sent(value_gradient.reshape(merged_shape)),
            "head",
            split_axis=1,
            concat_axis=2,
            tiled=True,
        ),
    )
    query_gradient = query_gradient.reshape(row_count, row_width)
    key_grad = key_grad.reshape(row_count, row_width)
    value_gradient = value_gradient.reshape(row_count, row_width)
    query_low_gradient = (ADAPTER_SCALE * last_product(query_gradient, query_up_weight)).astype(
        jnp.bfloat16
    )
    value_low_gradient = (ADAPTER_SCALE * last_product(value_gradient, value_up_weight)).astype(
        jnp.bfloat16
    )
    joined_grads = jnp.concatenate([query_gradient, key_grad, value_gradient], axis=1)
    normed_grad = (
        last_product(joined_grads, query_key_value_weight)
        + last_product(query_low_gradient, query_down_weight)
        + last_product(value_low_gradient, value_down_weight)
    )
    input_grad = hidden_grad + norm_back(flat_in, gain_one, shift_one, normed_grad)
    down_query = first_product(normed_rows, query_low_gradient)
    lifted_query = ADAPTER_SCALE * first_product(query_low_rank, query_gradient)
    down_value = first_product(normed_rows, value_low_gradient)
    lifted_value = ADAPTER_SCALE * first_product(value_low_rank, value_gradient)
    totals = lax.psum(
        (down_query, lifted_query, down_value, lifted_value, square_sums), ("dp", "head")
    )
    token_count = jnp.maximum(totals[4][2], 1.0)
    rms_values = jnp.stack(
        [
            jnp.sqrt(totals[4][0] / (token_count * row_width)),
            jnp.sqrt(totals[4][1] / (2.0 * token_count * row_width)),
        ]
    )
    return (
        output,
        input_grad.astype(jnp.bfloat16).reshape(block_input_rows.shape),
        totals[0],
        totals[1],
        totals[2],
        totals[3],
        rms_values,
    )


LOG2E = 1.4426950408889634
LN2 = 0.6931471805599453
TILE = 256
GROUP = 256
bf16 = jnp.bfloat16
f32 = jnp.float32
NT = (((1,), (1,)), ((), ()))
NN = (((1,), (0,)), ((), ()))
TN = (((0,), (0,)), ((), ()))
MESH = pl.DeviceIdType.MESH
MIB = 2**20


def dg(left, right, dims):
    return lax.dot_general(left, right, dims, preferred_element_type=f32)


def resident(shape):
    zeros = (0,) * len(shape)
    return pl.BlockSpec(shape, lambda *_: zeros, pipeline_mode=pl.Buffered(1))


def params(mib):
    return pltpu.CompilerParams(
        vmem_limit_bytes=mib * MIB, dimension_semantics=("arbitrary",)
    )


def norm_stats(rows):
    center = rows - jnp.mean(rows, axis=-1, keepdims=True)
    rs = lax.rsqrt(jnp.mean(center * center, axis=-1, keepdims=True) + EPSILON)
    return center * rs, rs


def norm_grad(unit, rs, gain, incoming):
    t = incoming * gain
    return (
        t - jnp.mean(t, axis=-1, keepdims=True) - unit * jnp.mean(t * unit, axis=-1, keepdims=True)
    ) * rs


def head_masks(x, heads, size):
    lane = lax.broadcasted_iota(jnp.int32, x.shape, 1)
    return [
        jnp.where((lane >= size * h) & (lane < size * (h + 1)), x, jnp.zeros_like(x))
        for h in range(heads)
    ]


def merge_heads(stacked, heads, size):
    rows = stacked.shape[0] // heads
    out = stacked[:rows]
    lane = lax.broadcasted_iota(jnp.int32, out.shape, 1)
    for h in range(1, heads):
        out = jnp.where(lane >= size * h, stacked[h * rows : (h + 1) * rows], out)
    return out


def column(line):
    return jnp.broadcast_to(line, (128, line.shape[1])).T


def entry_signal(peers):
    barrier = pltpu.get_barrier_semaphore()
    for peer in peers:
        pl.semaphore_signal(barrier, inc=1, device_id=peer, device_id_type=MESH)


def entry_wait(count):
    pl.semaphore_wait(pltpu.get_barrier_semaphore(), count)


def remote(src, dst, send_sem, recv_sem, peer):
    return pltpu.make_async_remote_copy(
        src_ref=src, dst_ref=dst, send_sem=send_sem, recv_sem=recv_sem, device_id=peer, device_id_type=MESH
    )


ANY = pl.BlockSpec(memory_space=pl.ANY)
VMEM = pl.BlockSpec(memory_space=pltpu.VMEM)


def attention_group(q_ref, k_ref, v_ref, o_ref, p_ref, s_sc, bias_sc, size, strip):
    length = q_ref.shape[0]
    heads = q_ref.shape[1] // size
    blocks = length // TILE

    def scores(i):
        masked = jnp.concatenate(head_masks(q_ref[i * TILE : (i + 1) * TILE, :], heads, size), 0)
        for j in range(i + 1):
            s_sc[i % 2, :, j * TILE : (j + 1) * TILE] = dg(masked, k_ref[j * TILE : (j + 1) * TILE, :], NT)

    def soft(i):
        n = (i + 1) * TILE
        for r in range(0, TILE, strip):
            for h in range(heads):
                at = h * TILE + r
                s = s_sc[i % 2, at : at + strip, 0:n] + bias_sc[i * TILE + r : i * TILE + r + strip, 0:n]
                e = jnp.exp2(s - jnp.max(s, axis=1, keepdims=True))
                total = jnp.sum(e, axis=1, keepdims=True)
                p_ref[h, i * TILE + r : i * TILE + r + strip, 0:n] = (e * (1.0 / total)).astype(bf16)

    def mix(i):
        n = (i + 1) * TILE
        probs = p_ref[:, i * TILE : n, 0:n].reshape(heads * TILE, n)
        o_ref[i * TILE : n, :] = merge_heads(dg(probs, v_ref[0:n, :], NN), heads, size).astype(bf16)

    for t in range(blocks + 2):
        if t < blocks:
            scores(t)
        if 0 <= t - 1 < blocks:
            soft(t - 1)
        if 0 <= t - 2 < blocks:
            mix(t - 2)


def line(ref):
    return ref[...].astype(f32).reshape(1, -1)


def open_kernel(
    x_ref, dy_ref, w_ref, mask_ref, start_ref, gain_ref, shift_ref, downq_ref, downv_ref, upq_ref, upv_ref,
    xs_ref, dys_ref, masks_ref, normed_ref, qkv_ref, ctx_ref, p_ref,
    x_sc, w_sc, mask_sc, normed_sc, qkv_sc, s_sc, bias_sc, first_sc,
    x_send, x_recv, y_send, y_recv, m_send, m_recv, local_sem,
    *, size, strip,
):
    slots, tile, width = x_ref.shape
    length = slots * tile
    half = length // 2
    groups = width // GROUP
    step = pl.program_id(0)
    group, me = lax.axis_index("dp"), lax.axis_index("head")
    mine = lax.rem(me, 2)
    near = me - mine
    far = slots // 2 - near
    beside = near + 1 - mine
    across = (far + mine, far + 1 - mine)
    peers = [(group, p) for p in (beside,) + across]

    def x_copy(k):
        return remote(x_ref.at[peers[k][1]], x_sc.at[me], x_send.at[k], x_recv.at[k], peers[k])

    def y_copy(k):
        return remote(dy_ref.at[peers[k][1]], dys_ref.at[me], y_send.at[k], y_recv.at[k], peers[k])

    def m_copy(k):
        return remote(mask_sc.at[peers[k][1]], masks_ref.at[me], m_send.at[k], m_recv.at[k], peers[k])

    def own_x():
        return pltpu.make_async_copy(x_ref.at[me], x_sc.at[me], local_sem.at[0])

    def own_y():
        return pltpu.make_async_copy(dy_ref.at[me], dys_ref.at[me], local_sem.at[1])

    def own_m():
        return pltpu.make_async_copy(mask_sc.at[me], masks_ref.at[me], local_sem.at[2])

    def weight():
        return pltpu.make_async_copy(w_ref, w_sc, local_sem.at[3])

    def save_x():
        return pltpu.make_async_copy(x_sc, xs_ref, local_sem.at[4])

    def save_normed():
        return pltpu.make_async_copy(normed_sc, normed_ref, local_sem.at[5])

    def save_qkv():
        return pltpu.make_async_copy(qkv_sc, qkv_ref, local_sem.at[6])

    @pl.when(step == 0)
    def _():
        entry_signal(peers)
        own_x().start()
        weight().start()
        own_y().start()
        for s in range(slots):
            mask_sc[s] = jnp.broadcast_to(mask_ref[s : s + 1, :].astype(f32), mask_sc.shape[1:])
        own_m().start()
        entry_wait(len(peers))
        for k in (1, 2, 0):
            x_copy(k).start()
        for k in range(3):
            m_copy(k).start()
        first_sc[...] = column(start_ref[pl.ds(me, 1), :])

        def bias(i, carry):
            here = pl.ds(pl.multiple_of(i * strip, strip), strip)
            keys = lax.broadcasted_iota(jnp.int32, (strip, length), 1)
            rows = lax.broadcasted_iota(jnp.int32, (strip, length), 0) + i * strip
            allowed = (keys >= first_sc[here, 0:1]) & (keys <= rows)
            bias_sc[here, :] = jnp.where(allowed, 0.0, NEGATIVE)
            return carry

        lax.fori_loop(0, length // strip, bias, 0)
        own_x().wait()
        x_copy(0).wait_recv()
        weight().wait()

    @pl.when(step == 1)
    def _():
        for k in (1, 2):
            x_copy(k).wait()
        for k in (1, 2, 0):
            y_copy(k).start()
        save_x().start()

    @pl.when(step < 2)
    def _():
        first = near + (far - near) * step
        rows = x_sc[pl.ds(first, 2)].reshape(half, width).astype(f32)
        unit, _ = norm_stats(rows)
        normed = (unit * line(gain_ref) + line(shift_ref)).astype(bf16)
        here = pl.ds(pl.multiple_of(first * tile, tile), half)
        normed_sc[here, :] = normed
        low_q = dg(normed, downq_ref[...], NT).astype(bf16)
        low_v = dg(normed, downv_ref[...], NT).astype(bf16)
        scale = size**-0.5 * LOG2E
        wide = 512
        for at in range(0, 3 * width, wide):
            cols = slice(at, at + wide)
            part = dg(normed, w_sc[:, cols], NN)
            if at < width:
                part = (part + ADAPTER_SCALE * dg(low_q, upq_ref[:, cols], NN)) * scale
            if at >= 2 * width:
                part = part + ADAPTER_SCALE * dg(low_v, upv_ref[:, at - 2 * width : at - 2 * width + wide], NN)
            qkv_sc[here, cols] = part.astype(bf16)

    @pl.when(step == 1)
    def _():
        save_normed().start()
        save_qkv().start()

    @pl.when(step >= 2)
    def _():
        g = step - 2

        def part(third):
            return qkv_sc.at[:, pl.ds(pl.multiple_of(third * width + g * GROUP, GROUP), GROUP)]

        attention_group(part(0), part(1), part(2), ctx_ref, p_ref, s_sc, bias_sc, size, strip)

    @pl.when(step == groups + 1)
    def _():
        x_copy(0).wait_send()
        for k in range(3):
            y_copy(k).wait()
            m_copy(k).wait()
        own_m().wait()
        own_y().wait()
        save_x().wait()
        save_normed().wait()
        save_qkv().wait()


def opening(x, dy, w, mask, start, gain, shift, downq, downv, upq, upv, size):
    slots, tile, width = x.shape
    length = slots * tile
    groups = width // GROUP
    per = GROUP // size
    dma = pltpu.SemaphoreType.DMA
    small = [mask, start, gain, shift, downq, downv, upq, upv]
    masks = (slots, 8, tile)
    return pl.pallas_call(
        functools.partial(open_kernel, size=size, strip=32),
        grid=(groups + 2,),
        in_specs=[ANY] * 3 + [resident(a.shape) for a in small],
        out_specs=[ANY] * 5 + [
            pl.BlockSpec((length, GROUP), lambda t: (0, jnp.maximum(t - 2, 0))),
            pl.BlockSpec((per, length, length), lambda t: (jnp.maximum(t - 2, 0), 0, 0)),
        ],
        out_shape=[
            jax.ShapeDtypeStruct(x.shape, bf16),
            jax.ShapeDtypeStruct(x.shape, bf16),
            jax.ShapeDtypeStruct(masks, f32),
            jax.ShapeDtypeStruct((length, width), bf16),
            jax.ShapeDtypeStruct((length, 3 * width), bf16),
            jax.ShapeDtypeStruct((length, width), bf16),
            jax.ShapeDtypeStruct((per * groups, length, length), bf16),
        ],
        scratch_shapes=[
            pltpu.VMEM(x.shape, bf16),
            pltpu.VMEM(w.shape, bf16),
            pltpu.VMEM(masks, f32),
            pltpu.VMEM((length, width), bf16),
            pltpu.VMEM((length, 3 * width), bf16),
            pltpu.VMEM((2, per * TILE, length), f32),
            pltpu.VMEM((length, length), f32),
            pltpu.VMEM((length, 128), jnp.int32),
            dma((3,)), dma((3,)), dma((3,)), dma((3,)), dma((3,)), dma((3,)), dma((7,)),
        ],
        compiler_params=pltpu.CompilerParams(
            collective_id=0, has_side_effects=True, vmem_limit_bytes=60 * MIB, dimension_semantics=("arbitrary",)
        ),
        name="opening",
    )(x, dy, w, *small)


def feed_kernel(
    x_ref, y_ref, ctx_ref, mask_ref, wo_hbm, wi_hbm, wf_hbm, gain_ref, shift_ref, bias_ref,
    out_ref, hg_ref, cg_ref, sums_ref, wo_ref, wi_ref, wf_ref, feed_sc, grad_sc, normed_sc, v_sc, g_sc, sem,
    *, step,
):
    blocks, tile, width = x_ref.shape
    rows = blocks * tile
    chunks = wi_ref.shape[1] // step
    first = pl.program_id(0) == 0

    def cols_of(c):
        return pl.ds(c * step if isinstance(c, int) else pl.multiple_of(c * step, step), step)

    def load_o():
        return pltpu.make_async_copy(wo_hbm, wo_ref, sem.at[2 * chunks])

    def load_i(c):
        return pltpu.make_async_copy(wi_hbm.at[:, cols_of(c)], wi_ref.at[:, cols_of(c)], sem.at[2 * c])

    def load_f(c):
        return pltpu.make_async_copy(wf_hbm.at[cols_of(c), :], wf_ref.at[cols_of(c), :], sem.at[2 * c + 1])

    @pl.when(first)
    def _():
        load_o().start()
        for c in range(chunks):
            load_i(c).start()
            load_f(c).start()
        load_o().wait()

    branch = dg(ctx_ref[...], wo_ref[...], NN)
    hidden = x_ref[...].reshape(rows, width).astype(f32) + branch
    unit, rs = norm_stats(hidden)
    gain = line(gain_ref)
    normed_sc[...] = (unit * gain + line(shift_ref)).astype(bf16)
    c0 = 0.7978845608028654
    c1 = c0 * 0.044715

    def enter(c, slot):
        @pl.when(first)
        def _():
            load_i(c).wait()
            load_f(c).wait()

        cols = cols_of(c)
        v_sc[slot] = dg(normed_sc[...], wi_ref[:, cols], NN) + bias_ref[cols].astype(f32).reshape(1, step)
        g_sc[slot] = dg(y_ref[...].reshape(rows, width), wf_ref[cols, :], NT)

    def leave(c, slot):
        v = v_sc[slot]
        square = v * v
        half = 0.5 * jnp.tanh(v * (c0 + c1 * square)) + 0.5
        act = v * half
        slope = half + act * (1.0 - half) * (2.0 * c0 + 6.0 * c1 * square)
        cols = cols_of(c)
        feed_sc[...] += dg(act.astype(bf16), wf_ref[cols, :], NN)
        grad_sc[...] += dg((slope * g_sc[slot]).astype(bf16), wi_ref[:, cols], NT)

    feed_sc[...] = jnp.zeros_like(feed_sc)
    grad_sc[...] = jnp.zeros_like(grad_sc)
    enter(0, 0)

    def pair(i, carry):
        enter(2 * i + 1, 1)
        leave(2 * i, 0)
        enter(2 * i + 2, 0)
        leave(2 * i + 1, 1)
        return carry

    lax.fori_loop(0, chunks // 2 - 1, pair, 0)
    enter(chunks - 1, 1)
    leave(chunks - 2, 0)
    leave(chunks - 1, 1)
    feed = feed_sc[...]
    result = hidden + feed
    out_ref[...] = result.astype(bf16).reshape(out_ref.shape)
    valid = jnp.concatenate([column(mask_ref[b, 0:1, :])[:, 0:1] for b in range(blocks)], 0)
    one = jnp.sum(valid * jnp.sum(result * result, axis=1, keepdims=True))
    two = jnp.sum(valid * jnp.sum(branch * branch + feed * feed, axis=1, keepdims=True))
    count = jnp.sum(valid)
    row = lax.broadcasted_iota(jnp.int32, sums_ref.shape, 0)
    col = lax.broadcasted_iota(jnp.int32, sums_ref.shape, 1)
    mine = jnp.where(col == 0, one, jnp.where(col == 1, two, jnp.where(col == 2, count, 0.0)))
    mine = jnp.where(row == 0, mine, 0.0)

    @pl.when(first)
    def _():
        sums_ref[...] = mine

    @pl.when(jnp.logical_not(first))
    def _():
        sums_ref[...] += mine

    dy = y_ref[...].reshape(rows, width).astype(f32)
    low = (dy + norm_grad(unit, rs, gain, grad_sc[...])).astype(bf16)
    hg_ref[...] = low
    cg_ref[...] = dg(low, wo_ref[...], NT).astype(bf16)


def feed(x, dy, context, mask, wo, gain, shift, wi, bias, wf):
    slots, tile, width = x.shape
    rows = slots * tile
    units = wi.shape[1]
    each = 2
    step = 512
    slab = pl.BlockSpec((each, tile, width), lambda i: (i, 0, 0))
    flat = pl.BlockSpec((each * tile, width), lambda i: (i, 0))
    return pl.pallas_call(
        functools.partial(feed_kernel, step=step),
        grid=(slots // each,),
        in_specs=[
            slab, slab, flat,
            pl.BlockSpec((each,) + mask.shape[1:], lambda i: (i, 0, 0)),
            ANY, ANY, ANY, resident(gain.shape), resident(shift.shape), resident(bias.shape),
        ],
        out_specs=[slab, flat, flat, pl.BlockSpec((8, width), lambda i: (0, 0))],
        out_shape=[
            jax.ShapeDtypeStruct(x.shape, bf16),
            jax.ShapeDtypeStruct((rows, width), bf16),
            jax.ShapeDtypeStruct((rows, width), bf16),
            jax.ShapeDtypeStruct((8, width), f32),
        ],
        scratch_shapes=[
            pltpu.VMEM(wo.shape, bf16), pltpu.VMEM(wi.shape, bf16), pltpu.VMEM(wf.shape, bf16),
            pltpu.VMEM((each * tile, width), f32), pltpu.VMEM((each * tile, width), f32),
            pltpu.VMEM((each * tile, width), bf16),
            pltpu.VMEM((2, each * tile, step), f32), pltpu.VMEM((2, each * tile, step), f32),
            pltpu.SemaphoreType.DMA((2 * (units // step) + 1,)),
        ],
        compiler_params=params(62),
        name="feed",
    )(x, dy, context, mask, wo, wi, wf, gain, shift, bias)


def attend_back_kernel(
    q_ref, k_ref, v_ref, g_ref, o_ref, p_ref, res_ref,
    dq_ref, dk_ref, dv_ref, out_ref,
    dp_sc, ds_sc, dk_sc, dv_sc, send, recv, local_sem,
    *, size, strip,
):
    length = q_ref.shape[0]
    heads = q_ref.shape[1] // size
    blocks = length // TILE
    scale = size**-0.5
    slots = res_ref.shape[0]
    group, me = lax.axis_index("dp"), lax.axis_index("head")
    peers = [(group, lax.rem(me + k, slots)) for k in range(1, slots)]
    grid_step = pl.program_id(0)

    def copy(k):
        return remote(res_ref.at[peers[k][1]], out_ref.at[me], send.at[k], recv.at[k], peers[k])

    def own():
        return pltpu.make_async_copy(res_ref.at[me], out_ref.at[me], local_sem)

    @pl.when(grid_step == 0)
    def _():
        entry_signal(peers)
        own().start()

    @pl.when(grid_step == 1)
    def _():
        entry_wait(len(peers))
        for k in range(len(peers)):
            copy(k).start()

    def stack(ref, i):
        return jnp.concatenate(head_masks(ref[i * TILE : (i + 1) * TILE, :], heads, size), 0)

    def prob_grads(i):
        masked = stack(g_ref, i)
        for j in range(i + 1):
            dp_sc[i % 2, :, j * TILE : (j + 1) * TILE] = dg(masked, v_ref[j * TILE : (j + 1) * TILE, :], NT)

    def score_grads(i):
        n = (i + 1) * TILE
        both = g_ref[i * TILE : n, :].astype(f32) * o_ref[i * TILE : n, :].astype(f32)
        for h in range(heads):
            for r in range(0, TILE, strip):
                at = h * TILE + r
                inner = jnp.sum(both[r : r + strip, size * h : size * (h + 1)], axis=1, keepdims=True)
                prob = p_ref[h, i * TILE + r : i * TILE + r + strip, 0:n].astype(f32)
                ds_sc[i % 2, at : at + strip, 0:n] = (prob * (dp_sc[i % 2, at : at + strip, 0:n] - inner)).astype(bf16)

    def products(i):
        n = (i + 1) * TILE
        dq = merge_heads(dg(ds_sc[i % 2, :, 0:n], k_ref[0:n, :], NN), heads, size)
        dq_ref[i * TILE : n, :] = (dq * scale).astype(bf16)
        grad4 = stack(g_ref, i)
        query4 = stack(q_ref, i)
        for j in range(i + 1):
            at = slice(j * TILE, (j + 1) * TILE)
            dv = dg(p_ref[:, i * TILE : n, at].reshape(heads * TILE, TILE), grad4, TN)
            dk = dg(ds_sc[i % 2, :, at], query4, TN)
            if i == j:
                dv_sc[at] = dv
                dk_sc[at] = dk
            else:
                dv_sc[at] += dv
                dk_sc[at] += dk

    for t in range(blocks + 2):
        if t < blocks:
            prob_grads(t)
        if 0 <= t - 1 < blocks:
            score_grads(t - 1)
        if 0 <= t - 2 < blocks:
            products(t - 2)
    dk_ref[...] = (dk_sc[...] * LN2).astype(bf16)
    dv_ref[...] = dv_sc[...].astype(bf16)

    @pl.when(grid_step == pl.num_programs(0) - 1)
    def _():
        own().wait()
        for k in range(len(peers)):
            copy(k).wait()


def attend_back_slot(qkv, grad, context, probs, result, size):
    length, wide = qkv.shape
    width = wide // 3
    groups = width // GROUP
    per = GROUP // size
    slots = result.shape[0]
    part = pl.BlockSpec((length, GROUP), lambda g: (0, g))
    dma = pltpu.SemaphoreType.DMA
    return pl.pallas_call(
        functools.partial(attend_back_kernel, size=size, strip=32),
        grid=(groups,),
        in_specs=[
            part,
            pl.BlockSpec((length, GROUP), lambda g: (0, g + groups)),
            pl.BlockSpec((length, GROUP), lambda g: (0, g + 2 * groups)),
            part,
            part,
            pl.BlockSpec((per, length, length), lambda g: (g, 0, 0)),
            ANY,
        ],
        out_specs=[part] * 3 + [ANY],
        out_shape=[jax.ShapeDtypeStruct((length, width), bf16)] * 3 + [jax.ShapeDtypeStruct(result.shape, bf16)],
        scratch_shapes=[
            pltpu.VMEM((2, per * TILE, length), f32),
            pltpu.VMEM((2, per * TILE, length), bf16),
            pltpu.VMEM((length, GROUP), f32),
            pltpu.VMEM((length, GROUP), f32),
            dma((slots - 1,)), dma((slots - 1,)), dma,
        ],
        compiler_params=pltpu.CompilerParams(
            collective_id=1, has_side_effects=True, vmem_limit_bytes=60 * MIB, dimension_semantics=("arbitrary",)
        ),
        name="attend_back",
    )(qkv, qkv, qkv, grad, context, probs, result)


def close_kernel(
    x_hbm, hg_hbm, dq_hbm, dk_hbm, dv_hbm, normed_hbm, w_hbm,
    gain_ref, downq_ref, downv_ref, upq_ref, upv_ref, sums_ref,
    out_ref, total_ref,
    x_sc, hg_sc, dq_sc, dk_sc, dv_sc, normed_sc, w_sc, low_sc, res_sc, sums, heard, parts, mean,
    load_sem, send, recv, local_sem, pair_send, pair_recv, part_send, part_recv, mean_send, mean_recv,
    *, sizes,
):
    slots, tile, width = x_sc.shape
    half = slots // 2 * tile
    rank = downq_ref.shape[0]
    group, me = lax.axis_index("dp"), lax.axis_index("head")
    mine = lax.rem(me, 2)
    near = me - mine
    far = slots // 2 - near
    beside = near + 1 - mine
    peers = [(group, p) for p in (far + mine, far + 1 - mine, beside)]
    rest = [(lax.rem(group + k, sizes[0]), me) for k in range(1, sizes[0])]
    lanes = width // sizes[0]
    arrays = [
        (dq_hbm, dq_sc), (dv_hbm, dv_sc), (normed_hbm, normed_sc), (dk_hbm, dk_sc), (x_hbm, x_sc), (hg_hbm, hg_sc)
    ]
    entry_signal(peers + rest)

    def load(a):
        src, dst = arrays[a]
        return pltpu.make_async_copy(src, dst, load_sem.at[a])

    def weight():
        return pltpu.make_async_copy(w_hbm, w_sc, local_sem.at[0])

    for a in range(len(arrays)):
        load(a).start()
    weight().start()
    for a in range(3):
        load(a).wait()

    def adapters(t, carry):
        at = pl.ds(2 * t, 2)
        dq = dq_sc[at].reshape(half, width)
        dv = dv_sc[at].reshape(half, width)
        normed = normed_sc[at].reshape(half, width)
        low_gq = (ADAPTER_SCALE * dg(dq, upq_ref[...], NT)).astype(bf16)
        low_gv = (ADAPTER_SCALE * dg(dv, upv_ref[...], NT)).astype(bf16)
        low_q = dg(normed, downq_ref[...], NT).astype(bf16)
        low_v = dg(normed, downv_ref[...], NT).astype(bf16)
        here = pl.ds(pl.multiple_of(t * half, half), half)
        low_sc[0, here, :] = low_gq
        low_sc[1, here, :] = low_gv
        sums[0, 0:rank] += dg(low_gq, normed, TN)
        sums[0, rank : 2 * rank] += dg(low_gv, normed, TN)
        sums[0, 2 * rank : 3 * rank] += ADAPTER_SCALE * dg(low_q, dq, TN)
        sums[0, 3 * rank : 4 * rank] += ADAPTER_SCALE * dg(low_v, dv, TN)
        return carry

    sums[0, 0 : 4 * rank] = jnp.zeros((4 * rank, width), f32)
    sums[0, 4 * rank :] = sums_ref[...]
    lax.fori_loop(0, 2, adapters, 0)

    def pair(at, peer):
        return remote(sums.at[at], heard.at[at], pair_send.at[at], pair_recv.at[at], peer)

    def block_of(d):
        return pl.ds(pl.multiple_of(d * lanes, lanes), lanes)

    def scatter(k):
        to = rest[k][0]
        return remote(
            sums.at[2, :, block_of(to)], parts.at[k], part_send.at[k], part_recv.at[k], rest[k]
        )

    def gather(k):
        return remote(
            mean, total_ref.at[:, block_of(group)], mean_send.at[k], mean_recv.at[k], rest[k]
        )

    def give(k):
        return remote(res_sc.at[peers[k][1]], out_ref.at[me], send.at[k], recv.at[k], peers[k])

    def keep():
        return pltpu.make_async_copy(res_sc.at[me], out_ref.at[me], local_sem.at[1])

    entry_wait(len(peers) + len(rest))
    pair(0, peers[0]).start()
    for a in range(3, len(arrays)):
        load(a).wait()
    weight().wait()

    def rows_back(t, carry):
        first = far + (near - far) * t
        at = pl.ds(first, 2)
        here = pl.ds(pl.multiple_of(first * tile, tile), half)
        normed_grad = (
            dg(dq_sc[at].reshape(half, width), w_sc[:, :width], NT)
            + dg(dk_sc[at].reshape(half, width), w_sc[:, width : 2 * width], NT)
            + dg(dv_sc[at].reshape(half, width), w_sc[:, 2 * width :], NT)
            + dg(low_sc[0, here, :], downq_ref[...], NN)
            + dg(low_sc[1, here, :], downv_ref[...], NN)
        )
        unit, rs = norm_stats(x_sc[at].reshape(half, width).astype(f32))
        grad = hg_sc[at].reshape(half, width).astype(f32) + norm_grad(unit, rs, line(gain_ref), normed_grad)
        res_sc[at] = grad.astype(bf16).reshape(2, tile, width)

        @pl.when(t == 0)
        def _():
            give(0).start()
            give(1).start()
            pair(0, peers[0]).wait()
            sums[1] = sums[0] + heard[0]
            pair(1, peers[2]).start()

        return carry

    lax.fori_loop(0, 2, rows_back, 0)
    give(2).start()
    keep().start()
    pair(1, peers[2]).wait()
    sums[2] = sums[1] + heard[1]
    for k in range(len(rest)):
        scatter(k).start()
    for k in range(len(rest)):
        scatter(k).wait()
    whole = sums[2, :, block_of(group)]
    for k in range(len(rest)):
        whole = whole + parts[k]
    mean[...] = whole
    total_ref[:, block_of(group)] = whole
    for k in range(len(rest)):
        gather(k).start()
    for k in range(len(rest)):
        gather(k).wait()
    keep().wait()
    for k in range(3):
        give(k).wait()


def closing(x, hidden_grad, dq, dk, dv, normed, w, gain, downq, downv, upq, upv, sums, sizes):
    slots, tile, width = x.shape
    rank = downq.shape[0]
    total = (4 * rank + 8, width)
    rest = sizes[0] - 1
    lanes = width // sizes[0]
    dma = pltpu.SemaphoreType.DMA

    def fold(a):
        return a.reshape(x.shape)

    return pl.pallas_call(
        functools.partial(close_kernel, sizes=sizes),
        in_specs=[ANY] * 7 + [VMEM] * 6,
        out_specs=[ANY, VMEM],
        out_shape=[jax.ShapeDtypeStruct(x.shape, bf16), jax.ShapeDtypeStruct(total, f32)],
        scratch_shapes=[pltpu.VMEM(x.shape, bf16)] * 6 + [
            pltpu.VMEM(w.shape, bf16),
            pltpu.VMEM((2, slots * tile, rank), bf16),
            pltpu.VMEM(x.shape, bf16),
            pltpu.VMEM((3,) + total, f32),
            pltpu.VMEM((2,) + total, f32),
            pltpu.VMEM((rest, total[0], lanes), f32),
            pltpu.VMEM((total[0], lanes), f32),
            dma((6,)), dma((3,)), dma((3,)), dma((2,)), dma((2,)), dma((2,)),
            dma((rest,)), dma((rest,)), dma((rest,)), dma((rest,)),
        ],
        compiler_params=pltpu.CompilerParams(collective_id=2, has_side_effects=True, vmem_limit_bytes=60 * MIB),
        name="closing",
    )(x, fold(hidden_grad), fold(dq), fold(dk), fold(dv), fold(normed), w, gain, downq, downv, upq, upv, sums)


def finish_kernel(total_ref, aq_ref, bq_ref, av_ref, bv_ref, rms_ref):
    rank, width = aq_ref.shape
    aq_ref[...] = total_ref[0:rank]
    av_ref[...] = total_ref[rank : 2 * rank]
    bq_ref[...] = total_ref[2 * rank : 3 * rank]
    bv_ref[...] = total_ref[3 * rank : 4 * rank]
    line = total_ref[4 * rank : 4 * rank + 1, 0:128]
    lane = lax.broadcasted_iota(jnp.int32, line.shape, 1)
    count = jnp.maximum(jnp.sum(jnp.where(lane == 2, line, 0.0)), 1.0)
    rms_ref[...] = jnp.sqrt(line / (jnp.where(lane == 0, 1.0, 2.0) * count * width))


def finish(total, rank):
    width = total.shape[1]
    small = jax.ShapeDtypeStruct((rank, width), f32)
    return pl.pallas_call(
        finish_kernel,
        in_specs=[VMEM],
        out_specs=[VMEM] * 5,
        out_shape=[small] * 4 + [jax.ShapeDtypeStruct((1, 128), f32)],
        name="finish",
    )(total)


def whole_slots(
    block_input_rows,
    document_starts,
    counted_mask,
    output_gradient,
    first_norm_gain,
    first_norm_bias,
    query_key_value_weight,
    query_down_weight,
    query_up_weight,
    value_down_weight,
    value_up_weight,
    attention_out_weight,
    second_norm_gain,
    second_norm_bias,
    feed_input_weight,
    feed_input_bias,
    feed_output_weight,
):
    sizes = (lax.axis_size("dp"), lax.axis_size("head"))
    size = block_input_rows.shape[-1] // H
    rank = query_down_weight.shape[1]
    downq = query_down_weight.T
    downv = value_down_weight.T
    x, dy, mask, normed, qkv, context, probs = opening(
        block_input_rows, output_gradient, query_key_value_weight, counted_mask, document_starts,
        first_norm_gain, first_norm_bias, downq, downv, query_up_weight, value_up_weight, size,
    )
    out, hidden_grad, context_grad, sums = feed(
        x, dy, context, mask, attention_out_weight, second_norm_gain, second_norm_bias,
        feed_input_weight, feed_input_bias, feed_output_weight,
    )
    dq, dk, dv, output = attend_back_slot(qkv, context_grad, context, probs, out, size)
    input_grad, total = closing(
        x, hidden_grad, dq, dk, dv, normed, query_key_value_weight, first_norm_gain, downq, downv,
        query_up_weight, value_up_weight, sums, sizes,
    )
    grad_aq, grad_bq, grad_av, grad_bv, rms = finish(total, rank)
    return output, input_grad, grad_aq.T, grad_bq, grad_av.T, grad_bv, rms[0, :2]


def body(*args):
    same = args[0].shape[0] == lax.axis_size("head")
    return whole_slots(*args) if same else shards(*args)


def solution(mesh):
    return jax.shard_map(
        body,
        mesh=mesh,
        in_specs=(
            P("dp", "head", None),
            P("dp", None),
            P("dp", "head"),
            P("dp", "head", None),
            P(),
            P(),
            P(),
            P(),
            P(),
            P(),
            P(),
            P(),
            P(),
            P(),
            P(),
            P(),
            P(),
        ),
        out_specs=(P("dp", "head", None), P("dp", "head", None), P(), P(), P(), P(), P()),
        check_vma=False,
    )
```

profile of v0, /device:TPU:0, one launch (start us, length us, event | category | flops | bytes accessed | tf_op | source)
XLA Modules:
  0.0 192.2 jit_solution(8395261547601113219)
XLA Ops:
  0.6 56.7 %opening.1 = (bf16[4,256,1024]{2,1,0:T(8,128)(2,1)}, bf16[4,256,1024]{2,1,0:T(8,128)(2,1)}, f32[4,8,256]{2,1,0:T(8,128)}, bf16[1024,1024]{1,0:T(8,128)(2,1)}, bf...) custom-call(bf16[4,256,1024]{2,1,0:T(8,128)(2,1)} %x_ref.1, ...), custom_call_target="tpu_custom_call" | custom-call | tf_op jit(solution)/shard_map/opening/pallas_call | solution.py:582
  57.4 54.1 %feed.1 = (bf16[4,256,1024]{2,1,0:T(8,128)(2,1)}, bf16[1024,1024]{1,0:T(8,128)(2,1)}, bf16[1024,1024]{1,0:T(8,128)(2,1)}, f32[8,1024]{1,0:T(8,128)}) custom-call(bf16[4,256,1024]{2,1,0:T(8,128)(2,1)} %get-tuple-element.30.x_ref.x_hbm, bf16[4,256,1024]{2,1,0:T(8,128)(2,1)} %get-tuple-element.31.y_ref, bf16[1024,1024]{1,0:T(8,128)(2,1)} %get-tuple-element.32.ctx_ref.o_ref, ...), custom_call_target="tpu_custom_call" | custom-call | tf_op jit(solution)/shard_map/feed/pallas_call | solution.py:724
  111.5 35.7 %attend_back.1 = (bf16[1024,1024]{1,0:T(8,128)(2,1)}, bf16[1024,1024]{1,0:T(8,128)(2,1)}, bf16[1024,1024]{1,0:T(8,128)(2,1)}, bf16[4,256,1024]{2,1,0:T(8,128)(2,1)}) custom-call(bf16[1024,3072]{1,0:T(8,128)(2,1)} %get-tuple-element.29.q_ref.k_ref.v_ref, bf16[1024,3072]{1,0:T(8,128)(2,1)} %get-tuple-element.29.q_ref.k_ref.v_ref, ...), custom_call_target="tpu_custom_call" | custom-call | tf_op jit(solution)/shard_map/attend_back/pallas_call | solution.py:843
  147.3 0.0 copy-start
  147.3 38.6 %closing.1 = (bf16[4,256,1024]{2,1,0:T(8,128)(2,1)}, f32[24,1024]{1,0:T(8,128)}) custom-call(bf16[4,256,1024]{2,1,0:T(8,128)(2,1)} %get-tuple-element.30.x_ref.x_hbm, bf16[4,256,1024]{2,1,0:T(8,128)(2,1)} %bitcast.12, bf16[4,256,1024]{2,1,0:T(8,128)(2,1)} %bitcast.13, bf16[4,256,1024]{2,1,0:T(8,128)(2,1)} %bitcast.14, bf16[4,256,1024]{2,1,0:T(8,128)(2,1)} %bitcast.15, ...), custom_call_target="tpu_custom_call" | custom-call | tf_op jit(solution)/shard_map/closing/pallas_call | solution.py:1018
  185.9 1.5 finish.1
  187.4 1.2 slice_bitcast_fusion
  188.6 0.0 copy-done
  188.6 0.0 copy-start.1
  188.6 1.3 copy.26
  189.9 1.0 copy-done.1
  190.9 1.3 copy.27
Async XLA Ops:
  147.3 41.3 %copy-start = (bf16[4,256,1024]{2,1,0:T(8,128)(2,1)S(1)}, bf16[4,256,1024]{2,1,0:T(8,128)(2,1)}, u32[]{:S(2)}) copy-start(bf16[4,256,1024]{2,1,0:T(8,128)(2,1)} %get-tuple-element.58) | copy-start | bytes 6291460
  188.6 2.3 %copy-start.1 = (bf16[4,256,1024]{2,1,0:T(8,128)(2,1)S(1)}, bf16[4,256,1024]{2,1,0:T(8,128)(2,1)}, u32[]{:S(2)}) copy-start(bf16[4,256,1024]{2,1,0:T(8,128)(2,1)} %get-tuple-element.59) | copy-start | bytes 6291460
where the time goes:
time: 193 us; the launch traced here: 192 us
  Pallas kernels  187 us (97%)
  local copies, waits for them, and re-layouts  4.84 us (3%)
    pallas_call x1, Pallas kernels, opening(): pl.pallas_call(functools.partial(open_kernel, size=size, strip=32), grid=...  56.7 us
    pallas_call x1, Pallas kernels, feed(): pl.pallas_call(functools.partial(feed_kernel, step=step), grid=(slots //...  54.1 us
    pallas_call x1, Pallas kernels, closing(): pl.pallas_call(functools.partial(close_kernel, sizes=sizes), in_specs=[AN...  38.6 us
    pallas_call x1, Pallas kernels, attend_back_slot(): pl.pallas_call(functools.partial(attend_back_kernel, size=size, strip=32)...  35.7 us

commit v1 on v0

--- a/solution.py
+++ b/solution.py
@@ -398,48 +398,35 @@
 VMEM = pl.BlockSpec(memory_space=pltpu.VMEM)
 
 
-def attention_group(q_ref, k_ref, v_ref, o_ref, p_ref, s_sc, bias_sc, size, strip):
-    length = q_ref.shape[0]
-    heads = q_ref.shape[1] // size
-    blocks = length // TILE
-
-    def scores(i):
-        masked = jnp.concatenate(head_masks(q_ref[i * TILE : (i + 1) * TILE, :], heads, size), 0)
-        for j in range(i + 1):
-            s_sc[i % 2, :, j * TILE : (j + 1) * TILE] = dg(masked, k_ref[j * TILE : (j + 1) * TILE, :], NT)
-
-    def soft(i):
-        n = (i + 1) * TILE
-        for r in range(0, TILE, strip):
-            for h in range(heads):
-                at = h * TILE + r
-                s = s_sc[i % 2, at : at + strip, 0:n] + bias_sc[i * TILE + r : i * TILE + r + strip, 0:n]
-                e = jnp.exp2(s - jnp.max(s, axis=1, keepdims=True))
-                total = jnp.sum(e, axis=1, keepdims=True)
-                p_ref[h, i * TILE + r : i * TILE + r + strip, 0:n] = (e * (1.0 / total)).astype(bf16)
-
-    def mix(i):
-        n = (i + 1) * TILE
-        probs = p_ref[:, i * TILE : n, 0:n].reshape(heads * TILE, n)
-        o_ref[i * TILE : n, :] = merge_heads(dg(probs, v_ref[0:n, :], NN), heads, size).astype(bf16)
-
-    for t in range(blocks + 2):
-        if t < blocks:
-            scores(t)
-        if 0 <= t - 1 < blocks:
-            soft(t - 1)
-        if 0 <= t - 2 < blocks:
-            mix(t - 2)
-
-
 def line(ref):
     return ref[...].astype(f32).reshape(1, -1)
 
 
+def rows_at(base, offset, count):
+    return pl.ds(pl.multiple_of(base + offset, TILE), count)
+
+
+def lanes_of(columns, width):
+    size = width // len(columns)
+    shape = (columns[0].shape[0], width)
+    lane = lax.broadcasted_iota(jnp.int32, shape, 1)
+    out = jnp.broadcast_to(columns[0], shape)
+    for h in range(1, len(columns)):
+        out = jnp.where(lane >= size * h, columns[h], out)
+    return out
+
+
+def pipelined(units, stages):
+    for t in range(len(units) + len(stages) - 1):
+        for b, stage in enumerate(stages):
+            if 0 <= t - b < len(units):
+                stage(t - b, units[t - b])
+
+
 def open_kernel(
     x_ref, dy_ref, w_ref, mask_ref, start_ref, gain_ref, shift_ref, downq_ref, downv_ref, upq_ref, upv_ref,
-    xs_ref, dys_ref, masks_ref, normed_ref, qkv_ref, ctx_ref, p_ref,
-    x_sc, w_sc, mask_sc, normed_sc, qkv_sc, s_sc, bias_sc, first_sc,
+    xs_ref, dys_ref, masks_ref, normed_ref, qkv_ref, ctx_ref, pd_ref, pc_ref, cd_ref, cc_ref,
+    x_sc, w_sc, mask_sc, normed_sc, qkv_sc, s_sc, diag_sc, cross_sc, first_sc, state, part,
     x_send, x_recv, y_send, y_recv, m_send, m_recv, local_sem,
     *, size, strip,
 ):
@@ -447,6 +434,7 @@
     length = slots * tile
     half = length // 2
     groups = width // GROUP
+    heads = GROUP // size
     step = pl.program_id(0)
     group, me = lax.axis_index("dp"), lax.axis_index("head")
     mine = lax.rem(me, 2)
@@ -504,18 +492,28 @@
 
         def bias(i, carry):
             here = pl.ds(pl.multiple_of(i * strip, strip), strip)
-            keys = lax.broadcasted_iota(jnp.int32, (strip, length), 1)
-            rows = lax.broadcasted_iota(jnp.int32, (strip, length), 0) + i * strip
+            base = half * lax.div(i * strip, half)
+            keys = lax.broadcasted_iota(jnp.int32, (strip, half), 1) + base
+            rows = lax.broadcasted_iota(jnp.int32, (strip, half), 0) + i * strip
             allowed = (keys >= first_sc[here, 0:1]) & (keys <= rows)
-            bias_sc[here, :] = jnp.where(allowed, 0.0, NEGATIVE)
+            diag_sc[here, :] = jnp.where(allowed, 0.0, NEGATIVE)
             return carry
 
         lax.fori_loop(0, length // strip, bias, 0)
+
+        def cross_bias(i, carry):
+            here = pl.ds(pl.multiple_of(i * strip, strip), strip)
+            keys = lax.broadcasted_iota(jnp.int32, (strip, half), 1)
+            rows = pl.ds(pl.multiple_of(half + i * strip, strip), strip)
+            cross_sc[here, :] = jnp.where(keys >= first_sc[rows, 0:1], 0.0, NEGATIVE)
+            return carry
+
+        lax.fori_loop(0, half // strip, cross_bias, 0)
         own_x().wait()
         x_copy(0).wait_recv()
         weight().wait()
 
-    @pl.when(step == 1)
+    @pl.when(step == groups + 1)
     def _():
         for k in (1, 2):
             x_copy(k).wait()
@@ -523,9 +521,9 @@
             y_copy(k).start()
         save_x().start()
 
-    @pl.when(step < 2)
-    def _():
-        first = near + (far - near) * step
+    @pl.when(lax.rem(step, groups + 1) == 0)
+    def _():
+        first = near + (far - near) * lax.div(step, groups + 1)
         rows = x_sc[pl.ds(first, 2)].reshape(half, width).astype(f32)
         unit, _ = norm_stats(rows)
         normed = (unit * line(gain_ref) + line(shift_ref)).astype(bf16)
@@ -537,28 +535,99 @@
         wide = 512
         for at in range(0, 3 * width, wide):
             cols = slice(at, at + wide)
-            part = dg(normed, w_sc[:, cols], NN)
+            piece = dg(normed, w_sc[:, cols], NN)
             if at < width:
-                part = (part + ADAPTER_SCALE * dg(low_q, upq_ref[:, cols], NN)) * scale
+                piece = (piece + ADAPTER_SCALE * dg(low_q, upq_ref[:, cols], NN)) * scale
             if at >= 2 * width:
-                part = part + ADAPTER_SCALE * dg(low_v, upv_ref[:, at - 2 * width : at - 2 * width + wide], NN)
-            qkv_sc[here, cols] = part.astype(bf16)
-
-    @pl.when(step == 1)
+                piece = piece + ADAPTER_SCALE * dg(low_v, upv_ref[:, at - 2 * width : at - 2 * width + wide], NN)
+            qkv_sc[here, cols] = piece.astype(bf16)
+
+    @pl.when(step == groups + 1)
     def _():
         save_normed().start()
         save_qkv().start()
 
-    @pl.when(step >= 2)
-    def _():
-        g = step - 2
-
-        def part(third):
-            return qkv_sc.at[:, pl.ds(pl.multiple_of(third * width + g * GROUP, GROUP), GROUP)]
-
-        attention_group(part(0), part(1), part(2), ctx_ref, p_ref, s_sc, bias_sc, size, strip)
-
-    @pl.when(step == groups + 1)
+    def attention(g, units):
+        def third(k):
+            return qkv_sc.at[:, pl.ds(pl.multiple_of(k * width + g * GROUP, GROUP), GROUP)]
+
+        q_ref, k_ref, v_ref = third(0), third(1), third(2)
+
+        def scores(at, unit):
+            i, n, q_base, k_base = unit[:4]
+            masked = jnp.concatenate(head_masks(q_ref[rows_at(q_base, i * TILE, TILE), :], heads, size), 0)
+            for j in range(0, n, TILE):
+                s_sc[at % 2, :, j : j + TILE] = dg(masked, k_ref[rows_at(k_base, j, TILE), :], NT)
+
+        def soft(at, unit):
+            i, n, q_base, _, bias, probs, (_, keep_m, keep_l, keep_row) = unit
+            tops, sums = [], []
+            for r in range(0, TILE, strip):
+                tops.append([])
+                sums.append([])
+                for h in range(heads):
+                    here = h * TILE + r
+                    s = s_sc[at % 2, here : here + strip, 0:n] + bias(i * TILE + r, n)
+                    top = jnp.max(s, axis=1, keepdims=True)
+                    e = jnp.exp2(s - top)
+                    tops[-1].append(top)
+                    sums[-1].append(jnp.sum(e, axis=1, keepdims=True))
+                    probs[h, i * TILE + r : i * TILE + r + strip, 0:n] = e.astype(bf16)
+                where = pl.ds(pl.multiple_of(keep_row + i * TILE + r, strip), strip)
+                keep_m[where, :] = lanes_of(tops[-1], GROUP)
+                keep_l[where, :] = lanes_of(sums[-1], GROUP)
+
+        def mix(at, unit):
+            i, n, _, k_base, _, probs, (keep_o, _, _, keep_row) = unit
+            stacked = probs[:, i * TILE : (i + 1) * TILE, 0:n].reshape(heads * TILE, n)
+            merged = merge_heads(dg(stacked, v_ref[rows_at(k_base, 0, n), :], NN), heads, size)
+            keep_o[rows_at(keep_row, i * TILE, TILE), :] = merged
+
+        pipelined(units, (scores, soft, mix))
+
+    def diag_units(g, base):
+        def bias(r, n):
+            return diag_sc[pl.ds(pl.multiple_of(base + r, strip), strip), 0:n]
+
+        kept = tuple(state.at[a, :, pl.ds(pl.multiple_of(g * GROUP, GROUP), GROUP)] for a in range(3))
+        return [
+            (i, (i + 1) * TILE, base, base, bias, pd_ref.at[0], kept + (base,)) for i in range(half // TILE)
+        ]
+
+    def cross_units(g):
+        def bias(r, n):
+            return cross_sc[r : r + strip, 0:n]
+
+        return [
+            (i, half, half, 0, bias, pc_ref, (part.at[0], part.at[1], part.at[2], 0)) for i in range(half // TILE)
+        ]
+
+    @pl.when((step > 0) & (step <= groups))
+    def _():
+        attention(step - 1, diag_units(step - 1, near * tile))
+
+    @pl.when(step > groups + 1)
+    def _():
+        g = step - groups - 2
+        attention(g, diag_units(g, far * tile) + cross_units(g))
+        cols = pl.ds(pl.multiple_of(g * GROUP, GROUP), GROUP)
+        inverse = 1.0 / state[2, 0:half, cols]
+        cd_ref[0:half] = inverse
+        ctx_ref[0:half] = (state[0, 0:half, cols] * inverse).astype(bf16)
+        for r in range(0, half, TILE):
+            high = slice(half + r, half + r + TILE)
+            here = slice(r, r + TILE)
+            top = jnp.maximum(state[1, high, cols], part[1, here])
+            weight_d = jnp.exp2(state[1, high, cols] - top)
+            weight_c = jnp.exp2(part[1, here] - top)
+            inverse = 1.0 / (weight_d * state[2, high, cols] + weight_c * part[2, here])
+            weight_d = weight_d * inverse
+            weight_c = weight_c * inverse
+            cd_ref[high] = weight_d
+            cc_ref[here] = weight_c
+            ctx_ref[high] = (state[0, high, cols] * weight_d + part[0, here] * weight_c).astype(bf16)
+
+    @pl.when(step == 2 * groups + 1)
     def _():
         x_copy(0).wait_send()
         for k in range(3):
@@ -574,18 +643,30 @@
 def opening(x, dy, w, mask, start, gain, shift, downq, downv, upq, upv, size):
     slots, tile, width = x.shape
     length = slots * tile
+    half = length // 2
     groups = width // GROUP
     per = GROUP // size
     dma = pltpu.SemaphoreType.DMA
     small = [mask, start, gain, shift, downq, downv, upq, upv]
     masks = (slots, 8, tile)
+
+    def late(t):
+        return jnp.maximum(t - groups - 2, 0)
+
+    def diag_at(t):
+        second = lax.div(t, groups + 2)
+        return second, jnp.where(second == 1, t - groups - 2, jnp.clip(t - 1, 0, groups - 1)), 0, 0
+
     return pl.pallas_call(
         functools.partial(open_kernel, size=size, strip=32),
-        grid=(groups + 2,),
+        grid=(2 * groups + 2,),
         in_specs=[ANY] * 3 + [resident(a.shape) for a in small],
         out_specs=[ANY] * 5 + [
-            pl.BlockSpec((length, GROUP), lambda t: (0, jnp.maximum(t - 2, 0))),
-            pl.BlockSpec((per, length, length), lambda t: (jnp.maximum(t - 2, 0), 0, 0)),
+            pl.BlockSpec((length, GROUP), lambda t: (0, late(t))),
+            pl.BlockSpec((1, per, half, half), diag_at),
+            pl.BlockSpec((per, half, half), lambda t: (late(t), 0, 0)),
+            pl.BlockSpec((length, GROUP), lambda t: (0, late(t))),
+            pl.BlockSpec((half, GROUP), lambda t: (0, late(t))),
         ],
         out_shape=[
             jax.ShapeDtypeStruct(x.shape, bf16),
@@ -594,7 +675,10 @@
             jax.ShapeDtypeStruct((length, width), bf16),
             jax.ShapeDtypeStruct((length, 3 * width), bf16),
             jax.ShapeDtypeStruct((length, width), bf16),
-            jax.ShapeDtypeStruct((per * groups, length, length), bf16),
+            jax.ShapeDtypeStruct((2, per * groups, half, half), bf16),
+            jax.ShapeDtypeStruct((per * groups, half, half), bf16),
+            jax.ShapeDtypeStruct((length, width), f32),
+            jax.ShapeDtypeStruct((half, width), f32),
         ],
         scratch_shapes=[
             pltpu.VMEM(x.shape, bf16),
@@ -602,13 +686,16 @@
             pltpu.VMEM(masks, f32),
             pltpu.VMEM((length, width), bf16),
             pltpu.VMEM((length, 3 * width), bf16),
-            pltpu.VMEM((2, per * TILE, length), f32),
-            pltpu.VMEM((length, length), f32),
+            pltpu.VMEM((2, per * TILE, half), f32),
+            pltpu.VMEM((length, half), f32),
+            pltpu.VMEM((half, half), f32),
             pltpu.VMEM((length, 128), jnp.int32),
+            pltpu.VMEM((3, length, width), f32),
+            pltpu.VMEM((3, half, GROUP), f32),
             dma((3,)), dma((3,)), dma((3,)), dma((3,)), dma((3,)), dma((3,)), dma((7,)),
         ],
         compiler_params=pltpu.CompilerParams(
-            collective_id=0, has_side_effects=True, vmem_limit_bytes=60 * MIB, dimension_semantics=("arbitrary",)
+            collective_id=0, has_side_effects=True, vmem_limit_bytes=62 * MIB, dimension_semantics=("arbitrary",)
         ),
         name="opening",
     )(x, dy, w, *small)
@@ -748,137 +835,24 @@
     )(x, dy, context, mask, wo, wi, wf, gain, shift, bias)
 
 
-def attend_back_kernel(
-    q_ref, k_ref, v_ref, g_ref, o_ref, p_ref, res_ref,
-    dq_ref, dk_ref, dv_ref, out_ref,
-    dp_sc, ds_sc, dk_sc, dv_sc, send, recv, local_sem,
-    *, size, strip,
-):
-    length = q_ref.shape[0]
-    heads = q_ref.shape[1] // size
-    blocks = length // TILE
-    scale = size**-0.5
-    slots = res_ref.shape[0]
-    group, me = lax.axis_index("dp"), lax.axis_index("head")
-    peers = [(group, lax.rem(me + k, slots)) for k in range(1, slots)]
-    grid_step = pl.program_id(0)
-
-    def copy(k):
-        return remote(res_ref.at[peers[k][1]], out_ref.at[me], send.at[k], recv.at[k], peers[k])
-
-    def own():
-        return pltpu.make_async_copy(res_ref.at[me], out_ref.at[me], local_sem)
-
-    @pl.when(grid_step == 0)
-    def _():
-        entry_signal(peers)
-        own().start()
-
-    @pl.when(grid_step == 1)
-    def _():
-        entry_wait(len(peers))
-        for k in range(len(peers)):
-            copy(k).start()
-
-    def stack(ref, i):
-        return jnp.concatenate(head_masks(ref[i * TILE : (i + 1) * TILE, :], heads, size), 0)
-
-    def prob_grads(i):
-        masked = stack(g_ref, i)
-        for j in range(i + 1):
-            dp_sc[i % 2, :, j * TILE : (j + 1) * TILE] = dg(masked, v_ref[j * TILE : (j + 1) * TILE, :], NT)
-
-    def score_grads(i):
-        n = (i + 1) * TILE
-        both = g_ref[i * TILE : n, :].astype(f32) * o_ref[i * TILE : n, :].astype(f32)
-        for h in range(heads):
-            for r in range(0, TILE, strip):
-                at = h * TILE + r
-                inner = jnp.sum(both[r : r + strip, size * h : size * (h + 1)], axis=1, keepdims=True)
-                prob = p_ref[h, i * TILE + r : i * TILE + r + strip, 0:n].astype(f32)
-                ds_sc[i % 2, at : at + strip, 0:n] = (prob * (dp_sc[i % 2, at : at + strip, 0:n] - inner)).astype(bf16)
-
-    def products(i):
-        n = (i + 1) * TILE
-        dq = merge_heads(dg(ds_sc[i % 2, :, 0:n], k_ref[0:n, :], NN), heads, size)
-        dq_ref[i * TILE : n, :] = (dq * scale).astype(bf16)
-        grad4 = stack(g_ref, i)
-        query4 = stack(q_ref, i)
-        for j in range(i + 1):
-            at = slice(j * TILE, (j + 1) * TILE)
-            dv = dg(p_ref[:, i * TILE : n, at].reshape(heads * TILE, TILE), grad4, TN)
-            dk = dg(ds_sc[i % 2, :, at], query4, TN)
-            if i == j:
-                dv_sc[at] = dv
-                dk_sc[at] = dk
-            else:
-                dv_sc[at] += dv
-                dk_sc[at] += dk
-
-    for t in range(blocks + 2):
-        if t < blocks:
-            prob_grads(t)
-        if 0 <= t - 1 < blocks:
-            score_grads(t - 1)
-        if 0 <= t - 2 < blocks:
-            products(t - 2)
-    dk_ref[...] = (dk_sc[...] * LN2).astype(bf16)
-    dv_ref[...] = dv_sc[...].astype(bf16)
-
-    @pl.when(grid_step == pl.num_programs(0) - 1)
-    def _():
-        own().wait()
-        for k in range(len(peers)):
-            copy(k).wait()
-
-
-def attend_back_slot(qkv, grad, context, probs, result, size):
-    length, wide = qkv.shape
-    width = wide // 3
-    groups = width // GROUP
-    per = GROUP // size
-    slots = result.shape[0]
-    part = pl.BlockSpec((length, GROUP), lambda g: (0, g))
-    dma = pltpu.SemaphoreType.DMA
-    return pl.pallas_call(
-        functools.partial(attend_back_kernel, size=size, strip=32),
-        grid=(groups,),
-        in_specs=[
-            part,
-            pl.BlockSpec((length, GROUP), lambda g: (0, g + groups)),
-            pl.BlockSpec((length, GROUP), lambda g: (0, g + 2 * groups)),
-            part,
-            part,
-            pl.BlockSpec((per, length, length), lambda g: (g, 0, 0)),
-            ANY,
-        ],
-        out_specs=[part] * 3 + [ANY],
-        out_shape=[jax.ShapeDtypeStruct((length, width), bf16)] * 3 + [jax.ShapeDtypeStruct(result.shape, bf16)],
-        scratch_shapes=[
-            pltpu.VMEM((2, per * TILE, length), f32),
-            pltpu.VMEM((2, per * TILE, length), bf16),
-            pltpu.VMEM((length, GROUP), f32),
-            pltpu.VMEM((length, GROUP), f32),
-            dma((slots - 1,)), dma((slots - 1,)), dma,
-        ],
-        compiler_params=pltpu.CompilerParams(
-            collective_id=1, has_side_effects=True, vmem_limit_bytes=60 * MIB, dimension_semantics=("arbitrary",)
-        ),
-        name="attend_back",
-    )(qkv, qkv, qkv, grad, context, probs, result)
-
-
 def close_kernel(
-    x_hbm, hg_hbm, dq_hbm, dk_hbm, dv_hbm, normed_hbm, w_hbm,
+    q_ref, k_ref, v_ref, g_ref, o_ref, cd_ref, cc_ref, pd_ref, pc_ref,
+    res_hbm, x_hbm, hg_hbm, normed_hbm, w_hbm,
     gain_ref, downq_ref, downv_ref, upq_ref, upv_ref, sums_ref,
-    out_ref, total_ref,
-    x_sc, hg_sc, dq_sc, dk_sc, dv_sc, normed_sc, w_sc, low_sc, res_sc, sums, heard, parts, mean,
-    load_sem, send, recv, local_sem, pair_send, pair_recv, part_send, part_recv, mean_send, mean_recv,
-    *, sizes,
+    result_ref, out_ref, total_ref,
+    dp_sc, ds_sc, inner_sc, do_sc, loc, near_sc, grads, x_sc, hg_sc, normed_sc, w_sc, res_sc,
+    sums, parts, chunk, heard, total_sc,
+    r_send, r_recv, send, recv, local_sem, part_send, part_recv, pair_send, pair_recv, mean_send, mean_recv,
+    *, size, strip, sizes,
 ):
     slots, tile, width = x_sc.shape
-    half = slots // 2 * tile
+    length = slots * tile
+    half = length // 2
+    groups = width // GROUP
+    heads = GROUP // size
     rank = downq_ref.shape[0]
+    step = pl.program_id(0)
+    last = 2 * groups + 1
     group, me = lax.axis_index("dp"), lax.axis_index("head")
     mine = lax.rem(me, 2)
     near = me - mine
@@ -887,153 +861,285 @@
     peers = [(group, p) for p in (far + mine, far + 1 - mine, beside)]
     rest = [(lax.rem(group + k, sizes[0]), me) for k in range(1, sizes[0])]
     lanes = width // sizes[0]
-    arrays = [
-        (dq_hbm, dq_sc), (dv_hbm, dv_sc), (normed_hbm, normed_sc), (dk_hbm, dk_sc), (x_hbm, x_sc), (hg_hbm, hg_sc)
-    ]
-    entry_signal(peers + rest)
-
-    def load(a):
-        src, dst = arrays[a]
-        return pltpu.make_async_copy(src, dst, load_sem.at[a])
-
-    def weight():
-        return pltpu.make_async_copy(w_hbm, w_sc, local_sem.at[0])
-
-    for a in range(len(arrays)):
-        load(a).start()
-    weight().start()
-    for a in range(3):
-        load(a).wait()
-
-    def adapters(t, carry):
-        at = pl.ds(2 * t, 2)
-        dq = dq_sc[at].reshape(half, width)
-        dv = dv_sc[at].reshape(half, width)
+
+    def own_result():
+        return pltpu.make_async_copy(res_hbm.at[me], result_ref.at[me], local_sem.at[0])
+
+    def result_copy(k):
+        return remote(res_hbm.at[peers[k][1]], result_ref.at[me], r_send.at[k], r_recv.at[k], peers[k])
+
+    def loads():
+        return [
+            pltpu.make_async_copy(src, dst, local_sem.at[1 + a])
+            for a, (src, dst) in enumerate([(x_hbm, x_sc), (hg_hbm, hg_sc), (normed_hbm, normed_sc), (w_hbm, w_sc)])
+        ]
+
+    @pl.when(step == 0)
+    def _():
+        entry_signal(peers + rest)
+        own_result().start()
+        for copy in loads():
+            copy.start()
+        sums[...] = jnp.zeros_like(sums)
+        sums[4 * rank :, :] = sums_ref[...]
+
+    @pl.when(step == 1)
+    def _():
+        entry_wait(len(peers) + len(rest))
+        for k in range(3):
+            result_copy(k).start()
+
+    def attention(units):
+        def stack(x):
+            return jnp.concatenate(head_masks(x, heads, size), 0)
+
+        def prob_grads(at, unit):
+            i, n, q_base, k_base, _, which, row = unit[:7]
+            grad = do_sc[which, rows_at(row, i * TILE, TILE), :]
+            masked = stack(grad)
+            for j in range(0, n, TILE):
+                dp_sc[at % 2, :, j : j + TILE] = dg(masked, v_ref[rows_at(k_base, j, TILE), :], NT)
+            both = (grad.astype(f32) * o_ref[rows_at(q_base, i * TILE, TILE), :].astype(f32)).astype(bf16)
+            inner_sc[at % 2] = dg(stack(both), jnp.ones((GROUP, 128), bf16), NN)
+
+        def score_grads(at, unit):
+            i, n, _, _, probs = unit[:5]
+            for h in range(heads):
+                for r in range(0, TILE, strip):
+                    here = h * TILE + r
+                    inner = jnp.concatenate([inner_sc[at % 2, here : here + strip, :]] * (n // 128), 1)
+                    prob = probs[h, i * TILE + r : i * TILE + r + strip, 0:n].astype(f32)
+                    ds = prob * (dp_sc[at % 2, here : here + strip, 0:n] - inner)
+                    ds_sc[at % 2, here : here + strip, 0:n] = ds.astype(bf16)
+
+        def products(at, unit):
+            i, n, q_base, k_base, probs, which, row, add = unit
+            query = rows_at(q_base, i * TILE, TILE)
+            ds = ds_sc[at % 2, :, 0:n]
+            dq = merge_heads(dg(ds, k_ref[rows_at(k_base, 0, n), :], NN), heads, size)
+            stacked = probs[:, i * TILE : (i + 1) * TILE, 0:n].reshape(heads * TILE, n)
+            dv = dg(stacked, stack(do_sc[which, rows_at(row, i * TILE, TILE), :]), TN)
+            dk = dg(ds, stack(q_ref[query, :]), TN)
+            if add:
+                loc[0, query, :] += dq
+                keys = rows_at(k_base, 0, n)
+                loc[1, keys, :] += dk
+                loc[2, keys, :] += dv
+            else:
+                loc[0, query, :] = dq
+                if i:
+                    keys = rows_at(k_base, 0, i * TILE)
+                    loc[1, keys, :] += dk[: i * TILE]
+                    loc[2, keys, :] += dv[: i * TILE]
+                loc[1, query, :] = dk[i * TILE :]
+                loc[2, query, :] = dv[i * TILE :]
+
+        pipelined(units, (prob_grads, score_grads, products))
+
+    def diag_units(base):
+        here = rows_at(base, 0, half)
+        do_sc[0] = (g_ref[here, :].astype(f32) * cd_ref[here, :]).astype(bf16)
+        return [(i, (i + 1) * TILE, base, base, pd_ref.at[0], 0, 0, False) for i in range(half // TILE)]
+
+    def cross_units():
+        do_sc[1] = (g_ref[half:, :].astype(f32) * cc_ref[...]).astype(bf16)
+        return [(i, half, half, 0, pc_ref, 1, 0, True) for i in range(half // TILE)]
+
+    scales = (size**-0.5, LN2, 1.0)
+
+    @pl.when(step < groups)
+    def _():
+        cols = pl.ds(pl.multiple_of(step * GROUP, GROUP), GROUP)
+        far_rows = rows_at(far * tile, 0, half)
+        near_rows = rows_at(near * tile, 0, half)
+        for a in range(3):
+            loc[a, near_rows, :] = jnp.zeros((half, GROUP), f32)
+        attention(diag_units(far * tile) + cross_units())
+        for a in range(3):
+            grads[a, far_rows, cols] = (loc[a, far_rows, :] * scales[a]).astype(bf16)
+            near_sc[a, :, cols] = loc[a, near_rows, :]
+
+    @pl.when((step > groups) & (step < last))
+    def _():
+        cols = pl.ds(pl.multiple_of((step - groups - 1) * GROUP, GROUP), GROUP)
+        near_rows = rows_at(near * tile, 0, half)
+        attention(diag_units(near * tile))
+        for a in range(3):
+            both = loc[a, near_rows, :] + near_sc[a, :, cols]
+            grads[a, near_rows, cols] = (both * scales[a]).astype(bf16)
+
+    def give(k):
+        return remote(res_sc.at[peers[k][1]], out_ref.at[me], send.at[k], recv.at[k], peers[k])
+
+    def give_part(p):
+        rows = pl.ds(p * (tile // 2), tile // 2)
+        return remote(
+            res_sc.at[peers[1][1], rows], out_ref.at[me, rows], send.at[1 + 2 * p], recv.at[1 + 2 * p], peers[1]
+        )
+
+    def keep():
+        return pltpu.make_async_copy(res_sc.at[me], out_ref.at[me], local_sem.at[5])
+
+    def block_of(d):
+        return pl.ds(pl.multiple_of(d * lanes, lanes), lanes)
+
+    def scatter(k):
+        return remote(sums.at[:, block_of(rest[k][0])], parts.at[k], part_send.at[k], part_recv.at[k], rest[k])
+
+    def pair(at, peer):
+        return remote(chunk.at[at], heard.at[at], pair_send.at[at], pair_recv.at[at], peer)
+
+    def gather(k):
+        return remote(chunk.at[2], total_sc.at[:, block_of(group)], mean_send.at[k], mean_recv.at[k], rest[k])
+
+    @pl.when(step == groups)
+    def _():
+        for copy in loads():
+            copy.wait()
+
+    @pl.when((step == groups) | (step == last))
+    def _():
+        first = far + (near - far) * lax.div(step, last)
+        at = pl.ds(first, 2)
+        here = pl.ds(pl.multiple_of(first * tile, tile), half)
+        dq, dk, dv = grads[0, here, :], grads[1, here, :], grads[2, here, :]
         normed = normed_sc[at].reshape(half, width)
         low_gq = (ADAPTER_SCALE * dg(dq, upq_ref[...], NT)).astype(bf16)
         low_gv = (ADAPTER_SCALE * dg(dv, upv_ref[...], NT)).astype(bf16)
         low_q = dg(normed, downq_ref[...], NT).astype(bf16)
         low_v = dg(normed, downv_ref[...], NT).astype(bf16)
-        here = pl.ds(pl.multiple_of(t * half, half), half)
-        low_sc[0, here, :] = low_gq
-        low_sc[1, here, :] = low_gv
-        sums[0, 0:rank] += dg(low_gq, normed, TN)
-        sums[0, rank : 2 * rank] += dg(low_gv, normed, TN)
-        sums[0, 2 * rank : 3 * rank] += ADAPTER_SCALE * dg(low_q, dq, TN)
-        sums[0, 3 * rank : 4 * rank] += ADAPTER_SCALE * dg(low_v, dv, TN)
-        return carry
-
-    sums[0, 0 : 4 * rank] = jnp.zeros((4 * rank, width), f32)
-    sums[0, 4 * rank :] = sums_ref[...]
-    lax.fori_loop(0, 2, adapters, 0)
-
-    def pair(at, peer):
-        return remote(sums.at[at], heard.at[at], pair_send.at[at], pair_recv.at[at], peer)
-
-    def block_of(d):
-        return pl.ds(pl.multiple_of(d * lanes, lanes), lanes)
-
-    def scatter(k):
-        to = rest[k][0]
-        return remote(
-            sums.at[2, :, block_of(to)], parts.at[k], part_send.at[k], part_recv.at[k], rest[k]
-        )
-
-    def gather(k):
-        return remote(
-            mean, total_ref.at[:, block_of(group)], mean_send.at[k], mean_recv.at[k], rest[k]
-        )
-
-    def give(k):
-        return remote(res_sc.at[peers[k][1]], out_ref.at[me], send.at[k], recv.at[k], peers[k])
-
-    def keep():
-        return pltpu.make_async_copy(res_sc.at[me], out_ref.at[me], local_sem.at[1])
-
-    entry_wait(len(peers) + len(rest))
-    pair(0, peers[0]).start()
-    for a in range(3, len(arrays)):
-        load(a).wait()
-    weight().wait()
-
-    def rows_back(t, carry):
-        first = far + (near - far) * t
-        at = pl.ds(first, 2)
-        here = pl.ds(pl.multiple_of(first * tile, tile), half)
+        sums[0:rank] += dg(low_gq, normed, TN)
+        sums[rank : 2 * rank] += dg(low_gv, normed, TN)
+        sums[2 * rank : 3 * rank] += ADAPTER_SCALE * dg(low_q, dq, TN)
+        sums[3 * rank : 4 * rank] += ADAPTER_SCALE * dg(low_v, dv, TN)
+
+        @pl.when(step == last)
+        def _():
+            for k in range(len(rest)):
+                scatter(k).start()
+
         normed_grad = (
-            dg(dq_sc[at].reshape(half, width), w_sc[:, :width], NT)
-            + dg(dk_sc[at].reshape(half, width), w_sc[:, width : 2 * width], NT)
-            + dg(dv_sc[at].reshape(half, width), w_sc[:, 2 * width :], NT)
-            + dg(low_sc[0, here, :], downq_ref[...], NN)
-            + dg(low_sc[1, here, :], downv_ref[...], NN)
+            dg(dq, w_sc[:, :width], NT)
+            + dg(dk, w_sc[:, width : 2 * width], NT)
+            + dg(dv, w_sc[:, 2 * width :], NT)
+            + dg(low_gq, downq_ref[...], NN)
+            + dg(low_gv, downv_ref[...], NN)
         )
         unit, rs = norm_stats(x_sc[at].reshape(half, width).astype(f32))
         grad = hg_sc[at].reshape(half, width).astype(f32) + norm_grad(unit, rs, line(gain_ref), normed_grad)
         res_sc[at] = grad.astype(bf16).reshape(2, tile, width)
 
-        @pl.when(t == 0)
-        def _():
-            give(0).start()
-            give(1).start()
-            pair(0, peers[0]).wait()
-            sums[1] = sums[0] + heard[0]
-            pair(1, peers[2]).start()
-
-        return carry
-
-    lax.fori_loop(0, 2, rows_back, 0)
-    give(2).start()
-    keep().start()
-    pair(1, peers[2]).wait()
-    sums[2] = sums[1] + heard[1]
-    for k in range(len(rest)):
-        scatter(k).start()
-    for k in range(len(rest)):
-        scatter(k).wait()
-    whole = sums[2, :, block_of(group)]
-    for k in range(len(rest)):
-        whole = whole + parts[k]
-    mean[...] = whole
-    total_ref[:, block_of(group)] = whole
-    for k in range(len(rest)):
-        gather(k).start()
-    for k in range(len(rest)):
-        gather(k).wait()
-    keep().wait()
-    for k in range(3):
-        give(k).wait()
-
-
-def closing(x, hidden_grad, dq, dk, dv, normed, w, gain, downq, downv, upq, upv, sums, sizes):
+    @pl.when(step == groups)
+    def _():
+        give(0).start()
+        give_part(0).start()
+
+    @pl.when(step == last)
+    def _():
+        give(2).start()
+        keep().start()
+        for k in range(len(rest)):
+            scatter(k).wait()
+        whole = sums[:, block_of(group)]
+        for k in range(len(rest)):
+            whole = whole + parts[k]
+        chunk[0] = whole
+        pair(0, peers[2]).start()
+        pair(0, peers[2]).wait()
+        chunk[1] = chunk[0] + heard[0]
+        pair(1, peers[0]).start()
+        give_part(1).start()
+        pair(1, peers[0]).wait()
+        whole = chunk[1] + heard[1]
+        chunk[2] = whole
+        total_sc[:, block_of(group)] = whole
+        for k in range(len(rest)):
+            gather(k).start()
+        for k in range(len(rest)):
+            gather(k).wait()
+        total_ref[...] = total_sc[...]
+        own_result().wait()
+        keep().wait()
+        for k in range(3):
+            result_copy(k).wait()
+        give(0).wait()
+        give(2).wait()
+        give_part(0).wait()
+        give_part(1).wait()
+
+
+def closing(
+    qkv, grad, context, cd, cc, pd, pc, result, x, hidden_grad, normed, w,
+    gain, downq, downv, upq, upv, sums, size, sizes,
+):
     slots, tile, width = x.shape
+    length = slots * tile
+    half = length // 2
+    groups = width // GROUP
+    per = GROUP // size
     rank = downq.shape[0]
     total = (4 * rank + 8, width)
     rest = sizes[0] - 1
     lanes = width // sizes[0]
     dma = pltpu.SemaphoreType.DMA
+    small = [gain, downq, downv, upq, upv, sums]
 
     def fold(a):
         return a.reshape(x.shape)
 
+    def of(t):
+        second = lax.div(t, groups + 1)
+        return jnp.minimum(t - second * (groups + 1), groups - 1)
+
+    def early(t):
+        return jnp.minimum(t, groups - 1)
+
+    def columns(third):
+        return pl.BlockSpec((length, GROUP), lambda t: (0, of(t) + third * groups))
+
     return pl.pallas_call(
-        functools.partial(close_kernel, sizes=sizes),
-        in_specs=[ANY] * 7 + [VMEM] * 6,
-        out_specs=[ANY, VMEM],
-        out_shape=[jax.ShapeDtypeStruct(x.shape, bf16), jax.ShapeDtypeStruct(total, f32)],
-        scratch_shapes=[pltpu.VMEM(x.shape, bf16)] * 6 + [
+        functools.partial(close_kernel, size=size, strip=32, sizes=sizes),
+        grid=(2 * groups + 2,),
+        in_specs=[
+            columns(0), columns(1), columns(2), columns(0), columns(0), columns(0),
+            pl.BlockSpec((half, GROUP), lambda t: (0, early(t))),
+            pl.BlockSpec((1, per, half, half), lambda t: (1 - lax.div(t, groups + 1), of(t), 0, 0)),
+            pl.BlockSpec((per, half, half), lambda t: (early(t), 0, 0)),
+        ]
+        + [ANY] * 5
+        + [resident(a.shape) for a in small],
+        out_specs=[ANY, ANY, pl.BlockSpec(total, lambda t: (0, 0))],
+        out_shape=[
+            jax.ShapeDtypeStruct(x.shape, bf16),
+            jax.ShapeDtypeStruct(x.shape, bf16),
+            jax.ShapeDtypeStruct(total, f32),
+        ],
+        scratch_shapes=[
+            pltpu.VMEM((2, per * TILE, half), f32),
+            pltpu.VMEM((2, per * TILE, half), bf16),
+            pltpu.VMEM((2, per * TILE, 128), f32),
+            pltpu.VMEM((2, half, GROUP), bf16),
+            pltpu.VMEM((3, length, GROUP), f32),
+            pltpu.VMEM((3, half, width), f32),
+            pltpu.VMEM((3, length, width), bf16),
+            pltpu.VMEM(x.shape, bf16),
+            pltpu.VMEM(x.shape, bf16),
+            pltpu.VMEM(x.shape, bf16),
             pltpu.VMEM(w.shape, bf16),
-            pltpu.VMEM((2, slots * tile, rank), bf16),
             pltpu.VMEM(x.shape, bf16),
-            pltpu.VMEM((3,) + total, f32),
-            pltpu.VMEM((2,) + total, f32),
+            pltpu.VMEM(total, f32),
             pltpu.VMEM((rest, total[0], lanes), f32),
-            pltpu.VMEM((total[0], lanes), f32),
-            dma((6,)), dma((3,)), dma((3,)), dma((2,)), dma((2,)), dma((2,)),
-            dma((rest,)), dma((rest,)), dma((rest,)), dma((rest,)),
+            pltpu.VMEM((3, total[0], lanes), f32),
+            pltpu.VMEM((2, total[0], lanes), f32),
+            pltpu.VMEM(total, f32),
+            dma((3,)), dma((3,)), dma((4,)), dma((4,)), dma((6,)),
+            dma((rest,)), dma((rest,)), dma((2,)), dma((2,)), dma((rest,)), dma((rest,)),
         ],
-        compiler_params=pltpu.CompilerParams(collective_id=2, has_side_effects=True, vmem_limit_bytes=60 * MIB),
+        compiler_params=pltpu.CompilerParams(
+            collective_id=1, has_side_effects=True, vmem_limit_bytes=62 * MIB, dimension_semantics=("arbitrary",)
+        ),
         name="closing",
-    )(x, fold(hidden_grad), fold(dq), fold(dk), fold(dv), fold(normed), w, gain, downq, downv, upq, upv, sums)
+    )(qkv, qkv, qkv, grad, context, cd, cc, pd, pc, result, x, fold(hidden_grad), fold(normed), w, *small)
 
 
 def finish_kernel(total_ref, aq_ref, bq_ref, av_ref, bv_ref, rms_ref):
@@ -1084,7 +1190,7 @@
     rank = query_down_weight.shape[1]
     downq = query_down_weight.T
     downv = value_down_weight.T
-    x, dy, mask, normed, qkv, context, probs = opening(
+    x, dy, mask, normed, qkv, context, pd, pc, cd, cc = opening(
         block_input_rows, output_gradient, query_key_value_weight, counted_mask, document_starts,
         first_norm_gain, first_norm_bias, downq, downv, query_up_weight, value_up_weight, size,
     )
@@ -1092,10 +1198,9 @@
         x, dy, context, mask, attention_out_weight, second_norm_gain, second_norm_bias,
         feed_input_weight, feed_input_bias, feed_output_weight,
     )
-    dq, dk, dv, output = attend_back_slot(qkv, context_grad, context, probs, out, size)
-    input_grad, total = closing(
-        x, hidden_grad, dq, dk, dv, normed, query_key_value_weight, first_norm_gain, downq, downv,
-        query_up_weight, value_up_weight, sums, sizes,
+    output, input_grad, total = closing(
+        qkv, context_grad, context, cd, cc, pd, pc, out, x, hidden_grad, normed, query_key_value_weight,
+        first_norm_gain, downq, downv, query_up_weight, value_up_weight, sums, size, sizes,
     )
     grad_aq, grad_bq, grad_av, grad_bv, rms = finish(total, rank)
     return output, input_grad, grad_aq.T, grad_bq, grad_av.T, grad_bv, rms[0, :2]

time: 193 us -> 180 us (0.933)
  Pallas kernels: 187 us -> 173 us
    pallas_call x2 -> x1, Pallas kernels: 74.3 us -> 61.6 us  [closing(): pl.pallas_call(functools.partial(close_kernel, size=size, strip=32, sizes...]
    unnamed x6 -> x4, local copies, waits for them, and re-layouts: 3.67 us -> 4.55 us
where the time goes in v1:
time: 180 us
  Pallas kernels  173 us (96%)
  local copies, waits for them, and re-layouts  5.72 us (3%)
    pallas_call x1, Pallas kernels, closing(): pl.pallas_call(functools.partial(close_kernel, size=size, strip=32, sizes...  61.6 us
    pallas_call x1, Pallas kernels, opening(): pl.pallas_call(functools.partial(open_kernel, size=size, strip=32), grid=...  56 us
    pallas_call x1, Pallas kernels, feed(): pl.pallas_call(functools.partial(feed_kernel, step=step), grid=(slots //...  54.1 us
    unnamed x4, local copies, waits for them, and re-layouts  4.55 us

profile of v1, /device:TPU:0, one launch (start us, length us, event | category | flops | bytes accessed | tf_op | source)
XLA Modules:
  0.0 179.7 jit_solution(3089773770789621320)
XLA Ops:
  0.6 56.0 %opening.1 = (bf16[4,256,1024]{2,1,0:T(8,128)(2,1)}, bf16[4,256,1024]{2,1,0:T(8,128)(2,1)}, f32[4,8,256]{2,1,0:T(8,128)}, bf16[1024,1024]{1,0:T(8,128)(2,1)}, bf...) custom-call(bf16[4,256,1024]{2,1,0:T(8,128)(2,1)} %x_ref.1, ...), custom_call_target="tpu_custom_call" | custom-call | tf_op jit(solution)/shard_map/opening/pallas_call | solution.py:660
  56.7 54.1 %feed.1 = (bf16[4,256,1024]{2,1,0:T(8,128)(2,1)}, bf16[1024,1024]{1,0:T(8,128)(2,1)}, bf16[1024,1024]{1,0:T(8,128)(2,1)}, f32[8,1024]{1,0:T(8,128)}) custom-call(bf16[4,256,1024]{2,1,0:T(8,128)(2,1)} %get-tuple-element.30.x_ref.x_hbm, bf16[4,256,1024]{2,1,0:T(8,128)(2,1)} %get-tuple-element.31.y_ref, bf16[1024,1024]{1,0:T(8,128)(2,1)} %get-tuple-element.32.ctx_ref.o_ref, ...), custom_call_target="tpu_custom_call" | custom-call | tf_op jit(solution)/shard_map/feed/pallas_call | solution.py:811
  110.8 61.6 %closing.1 = (bf16[4,256,1024]{2,1,0:T(8,128)(2,1)}, bf16[4,256,1024]{2,1,0:T(8,128)(2,1)}, f32[24,1024]{1,0:T(8,128)}) custom-call(bf16[1024,3072]{1,0:T(8,128)(2,1)} %get-tuple-element.29.q_ref.k_ref.v_ref, bf16[1024,3072]{1,0:T(8,128)(2,1)} %get-tuple-element.29.q_ref.k_ref.v_ref, bf16[1024,3072]{1,0:T(8,128)(2,1)} %get-tuple-element.29.q_ref.k_ref.v_ref, ...), custom_call_target="tpu_custom_call" | custom-call | tf_op jit(solution)/shard_map/closing/pallas_call | solution.py:1100
  172.5 1.5 finish.1
  174.0 1.2 slice_bitcast_fusion
  175.2 0.0 copy-start
  175.2 3.2 %copy.26 = bf16[4,256,1024]{2,1,0:T(8,128)(2,1)} copy(bf16[4,256,1024]{2,1,0:T(8,128)(2,1)} %get-tuple-element.58) | data formatting | bytes 4194304
  178.4 0.0 copy-done
  178.4 1.3 copy.27
Async XLA Ops:
  175.2 3.2 %copy-start = (bf16[4,256,1024]{2,1,0:T(8,128)(2,1)S(1)}, bf16[4,256,1024]{2,1,0:T(8,128)(2,1)}, u32[]{:S(2)}) copy-start(bf16[4,256,1024]{2,1,0:T(8,128)(2,1)} %get-tuple-element.59) | copy-start | bytes 6291460

commit v2 on v1

--- a/solution.py
+++ b/solution.py
@@ -426,7 +426,7 @@
 def open_kernel(
     x_ref, dy_ref, w_ref, mask_ref, start_ref, gain_ref, shift_ref, downq_ref, downv_ref, upq_ref, upv_ref,
     xs_ref, dys_ref, masks_ref, normed_ref, qkv_ref, ctx_ref, pd_ref, pc_ref, cd_ref, cc_ref,
-    x_sc, w_sc, mask_sc, normed_sc, qkv_sc, s_sc, diag_sc, cross_sc, first_sc, state, part,
+    x_sc, y_sc, w_sc, mask_sc, normed_sc, qkv_sc, s_sc, diag_sc, cross_sc, first_sc, near_sc, state, part,
     x_send, x_recv, y_send, y_recv, m_send, m_recv, local_sem,
     *, size, strip,
 ):
@@ -436,6 +436,7 @@
     groups = width // GROUP
     heads = GROUP // size
     step = pl.program_id(0)
+    middle = groups + 1
     group, me = lax.axis_index("dp"), lax.axis_index("head")
     mine = lax.rem(me, 2)
     near = me - mine
@@ -448,7 +449,8 @@
         return remote(x_ref.at[peers[k][1]], x_sc.at[me], x_send.at[k], x_recv.at[k], peers[k])
 
     def y_copy(k):
-        return remote(dy_ref.at[peers[k][1]], dys_ref.at[me], y_send.at[k], y_recv.at[k], peers[k])
+        landing = y_sc.at[mine] if k == 0 else dys_ref.at[me]
+        return remote(dy_ref.at[peers[k][1]], landing, y_send.at[k], y_recv.at[k], peers[k])
 
     def m_copy(k):
         return remote(mask_sc.at[peers[k][1]], masks_ref.at[me], m_send.at[k], m_recv.at[k], peers[k])
@@ -457,7 +459,7 @@
         return pltpu.make_async_copy(x_ref.at[me], x_sc.at[me], local_sem.at[0])
 
     def own_y():
-        return pltpu.make_async_copy(dy_ref.at[me], dys_ref.at[me], local_sem.at[1])
+        return pltpu.make_async_copy(dy_ref.at[me], y_sc.at[mine], local_sem.at[1])
 
     def own_m():
         return pltpu.make_async_copy(mask_sc.at[me], masks_ref.at[me], local_sem.at[2])
@@ -467,6 +469,9 @@
 
     def save_x():
         return pltpu.make_async_copy(x_sc, xs_ref, local_sem.at[4])
+
+    def save_y():
+        return pltpu.make_async_copy(y_sc, dys_ref.at[pl.ds(near, 2)], local_sem.at[7])
 
     def save_normed():
         return pltpu.make_async_copy(normed_sc, normed_ref, local_sem.at[5])
@@ -509,23 +514,25 @@
             return carry
 
         lax.fori_loop(0, half // strip, cross_bias, 0)
+        y_copy(0).start()
         own_x().wait()
         x_copy(0).wait_recv()
         weight().wait()
 
     @pl.when(step == groups + 1)
     def _():
-        for k in (1, 2):
-            x_copy(k).wait()
-        for k in (1, 2, 0):
-            y_copy(k).start()
+        own_y().wait()
+        y_copy(0).wait_recv()
+        save_y().start()
+        x_copy(1).wait()
+        x_copy(2).wait()
+        y_copy(1).start()
         save_x().start()
 
-    @pl.when(lax.rem(step, groups + 1) == 0)
-    def _():
-        first = near + (far - near) * lax.div(step, groups + 1)
-        rows = x_sc[pl.ds(first, 2)].reshape(half, width).astype(f32)
-        unit, _ = norm_stats(rows)
+    @pl.when(lax.rem(step, middle) == 0)
+    def _():
+        first = near + (far - near) * lax.div(step, middle)
+        unit, _ = norm_stats(x_sc[pl.ds(first, 2)].reshape(half, width).astype(f32))
         normed = (unit * line(gain_ref) + line(shift_ref)).astype(bf16)
         here = pl.ds(pl.multiple_of(first * tile, tile), half)
         normed_sc[here, :] = normed
@@ -542,7 +549,7 @@
                 piece = piece + ADAPTER_SCALE * dg(low_v, upv_ref[:, at - 2 * width : at - 2 * width + wide], NN)
             qkv_sc[here, cols] = piece.astype(bf16)
 
-    @pl.when(step == groups + 1)
+    @pl.when(step == middle)
     def _():
         save_normed().start()
         save_qkv().start()
@@ -585,16 +592,14 @@
 
         pipelined(units, (scores, soft, mix))
 
-    def diag_units(g, base):
+    def diag_units(base, keep, keep_row):
         def bias(r, n):
             return diag_sc[pl.ds(pl.multiple_of(base + r, strip), strip), 0:n]
 
-        kept = tuple(state.at[a, :, pl.ds(pl.multiple_of(g * GROUP, GROUP), GROUP)] for a in range(3))
-        return [
-            (i, (i + 1) * TILE, base, base, bias, pd_ref.at[0], kept + (base,)) for i in range(half // TILE)
-        ]
-
-    def cross_units(g):
+        kept = (*keep, keep_row)
+        return [(i, (i + 1) * TILE, base, base, bias, pd_ref.at[0], kept) for i in range(half // TILE)]
+
+    def cross_units():
         def bias(r, n):
             return cross_sc[r : r + strip, 0:n]
 
@@ -604,38 +609,44 @@
 
     @pl.when((step > 0) & (step <= groups))
     def _():
-        attention(step - 1, diag_units(step - 1, near * tile))
-
-    @pl.when(step > groups + 1)
-    def _():
-        g = step - groups - 2
-        attention(g, diag_units(g, far * tile) + cross_units(g))
+        cols = pl.ds(pl.multiple_of((step - 1) * GROUP, GROUP), GROUP)
+        attention(step - 1, diag_units(near * tile, [near_sc.at[a, :, cols] for a in range(3)], 0))
+
+    @pl.when(step > middle)
+    def _():
+        g = step - middle - 1
         cols = pl.ds(pl.multiple_of(g * GROUP, GROUP), GROUP)
-        inverse = 1.0 / state[2, 0:half, cols]
+        near_rows = rows_at(near * tile, 0, half)
+        for a in range(3):
+            state[a, near_rows, :] = near_sc[a, :, cols]
+        far_units = diag_units(far * tile, [state.at[a] for a in range(3)], far * tile)
+        attention(g, far_units + cross_units())
+        inverse = 1.0 / state[2, 0:half]
         cd_ref[0:half] = inverse
-        ctx_ref[0:half] = (state[0, 0:half, cols] * inverse).astype(bf16)
+        ctx_ref[0:half] = (state[0, 0:half] * inverse).astype(bf16)
         for r in range(0, half, TILE):
             high = slice(half + r, half + r + TILE)
             here = slice(r, r + TILE)
-            top = jnp.maximum(state[1, high, cols], part[1, here])
-            weight_d = jnp.exp2(state[1, high, cols] - top)
+            top = jnp.maximum(state[1, high], part[1, here])
+            weight_d = jnp.exp2(state[1, high] - top)
             weight_c = jnp.exp2(part[1, here] - top)
-            inverse = 1.0 / (weight_d * state[2, high, cols] + weight_c * part[2, here])
+            inverse = 1.0 / (weight_d * state[2, high] + weight_c * part[2, here])
             weight_d = weight_d * inverse
             weight_c = weight_c * inverse
             cd_ref[high] = weight_d
             cc_ref[here] = weight_c
-            ctx_ref[high] = (state[0, high, cols] * weight_d + part[0, here] * weight_c).astype(bf16)
-
-    @pl.when(step == 2 * groups + 1)
+            ctx_ref[high] = (state[0, high] * weight_d + part[0, here] * weight_c).astype(bf16)
+
+    @pl.when(step == middle + groups)
     def _():
         x_copy(0).wait_send()
+        y_copy(0).wait_send()
+        y_copy(1).wait()
         for k in range(3):
-            y_copy(k).wait()
             m_copy(k).wait()
         own_m().wait()
-        own_y().wait()
         save_x().wait()
+        save_y().wait()
         save_normed().wait()
         save_qkv().wait()
 
@@ -650,16 +661,18 @@
     small = [mask, start, gain, shift, downq, downv, upq, upv]
     masks = (slots, 8, tile)
 
+    middle = groups + 1
+
     def late(t):
-        return jnp.maximum(t - groups - 2, 0)
+        return jnp.maximum(t - middle - 1, 0)
 
     def diag_at(t):
-        second = lax.div(t, groups + 2)
-        return second, jnp.where(second == 1, t - groups - 2, jnp.clip(t - 1, 0, groups - 1)), 0, 0
+        second = lax.div(t, middle + 1)
+        return second, jnp.where(second == 1, t - middle - 1, jnp.clip(t - 1, 0, groups - 1)), 0, 0
 
     return pl.pallas_call(
         functools.partial(open_kernel, size=size, strip=32),
-        grid=(2 * groups + 2,),
+        grid=(middle + groups + 1,),
         in_specs=[ANY] * 3 + [resident(a.shape) for a in small],
         out_specs=[ANY] * 5 + [
             pl.BlockSpec((length, GROUP), lambda t: (0, late(t))),
@@ -682,6 +695,7 @@
         ],
         scratch_shapes=[
             pltpu.VMEM(x.shape, bf16),
+            pltpu.VMEM((2, tile, width), bf16),
             pltpu.VMEM(w.shape, bf16),
             pltpu.VMEM(masks, f32),
             pltpu.VMEM((length, width), bf16),
@@ -690,9 +704,10 @@
             pltpu.VMEM((length, half), f32),
             pltpu.VMEM((half, half), f32),
             pltpu.VMEM((length, 128), jnp.int32),
-            pltpu.VMEM((3, length, width), f32),
+            pltpu.VMEM((3, half, width), f32),
+            pltpu.VMEM((3, length, GROUP), f32),
             pltpu.VMEM((3, half, GROUP), f32),
-            dma((3,)), dma((3,)), dma((3,)), dma((3,)), dma((3,)), dma((3,)), dma((7,)),
+            dma((3,)), dma((3,)), dma((3,)), dma((3,)), dma((3,)), dma((3,)), dma((8,)),
         ],
         compiler_params=pltpu.CompilerParams(
             collective_id=0, has_side_effects=True, vmem_limit_bytes=62 * MIB, dimension_semantics=("arbitrary",)
@@ -702,68 +717,126 @@
 
 
 def feed_kernel(
-    x_ref, y_ref, ctx_ref, mask_ref, wo_hbm, wi_hbm, wf_hbm, gain_ref, shift_ref, bias_ref,
-    out_ref, hg_ref, cg_ref, sums_ref, wo_ref, wi_ref, wf_ref, feed_sc, grad_sc, normed_sc, v_sc, g_sc, sem,
+    x_hbm, y_hbm, dy_hbm, ctx_hbm, wo_hbm, wi_hbm, wf_hbm, mask_ref, gain_ref, shift_ref, bias_ref,
+    out_hbm, hg_hbm, cg_hbm, sums_ref,
+    x_sc, y_sc, ctx_sc, wo_ref, wi_ref, wf_ref, normed, feed_sc, grad_sc, v_sc, g_sc,
+    out_sc, hg_sc, cg_sc, load_sem, chunk_sem, save_sem, y_send, y_recv,
     *, step,
 ):
-    blocks, tile, width = x_ref.shape
-    rows = blocks * tile
+    slots, tile, width = x_hbm.shape
+    rows = slots // 2 * tile
     chunks = wi_ref.shape[1] // step
-    first = pl.program_id(0) == 0
+    group, me = lax.axis_index("dp"), lax.axis_index("head")
+    mine = lax.rem(me, 2)
+    near = me - mine
+    far = slots // 2 - near
+    across = (far + mine, far + 1 - mine)
+    peer = (group, across[1])
+    half = pl.program_id(0)
+    first = half == 0
+
+    def base(h):
+        return near + (far - near) * h
+
+    def slabs(ref, h):
+        return ref.at[pl.ds(base(h), 2)]
+
+    def load_x(h):
+        return pltpu.make_async_copy(slabs(x_hbm, h), x_sc.at[h], load_sem.at[h, 0])
+
+    def load_ctx(h):
+        return pltpu.make_async_copy(slabs(ctx_hbm, h), ctx_sc.at[h], load_sem.at[h, 1])
+
+    def load_y(h):
+        if h == 0:
+            return pltpu.make_async_copy(slabs(y_hbm, 0), y_sc.at[0], load_sem.at[0, 2])
+        return pltpu.make_async_copy(y_hbm.at[across[0]], y_sc.at[1, mine], load_sem.at[1, 2])
+
+    def take_y():
+        return remote(dy_hbm.at[across[1]], y_sc.at[1, mine], y_send, y_recv, peer)
+
+    def load_o():
+        return pltpu.make_async_copy(wo_hbm, wo_ref, load_sem.at[0, 3])
 
     def cols_of(c):
         return pl.ds(c * step if isinstance(c, int) else pl.multiple_of(c * step, step), step)
 
-    def load_o():
-        return pltpu.make_async_copy(wo_hbm, wo_ref, sem.at[2 * chunks])
-
     def load_i(c):
-        return pltpu.make_async_copy(wi_hbm.at[:, cols_of(c)], wi_ref.at[:, cols_of(c)], sem.at[2 * c])
+        return pltpu.make_async_copy(wi_hbm.at[:, cols_of(c)], wi_ref.at[:, cols_of(c)], chunk_sem.at[0, c])
 
     def load_f(c):
-        return pltpu.make_async_copy(wf_hbm.at[cols_of(c), :], wf_ref.at[cols_of(c), :], sem.at[2 * c + 1])
+        return pltpu.make_async_copy(wf_hbm.at[cols_of(c), :], wf_ref.at[cols_of(c), :], chunk_sem.at[1, c])
 
     @pl.when(first)
     def _():
+        entry_signal([peer])
         load_o().start()
+        load_ctx(0).start()
+        load_x(0).start()
         for c in range(chunks):
             load_i(c).start()
             load_f(c).start()
+            if c == 1:
+                load_y(0).start()
+                load_y(1).start()
+                load_ctx(1).start()
+                load_x(1).start()
+        sums_ref[...] = jnp.zeros_like(sums_ref)
         load_o().wait()
-
-    branch = dg(ctx_ref[...], wo_ref[...], NN)
-    hidden = x_ref[...].reshape(rows, width).astype(f32) + branch
-    unit, rs = norm_stats(hidden)
+        load_ctx(0).wait()
+        load_x(0).wait()
+
     gain = line(gain_ref)
-    normed_sc[...] = (unit * gain + line(shift_ref)).astype(bf16)
     c0 = 0.7978845608028654
     c1 = c0 * 0.044715
+    branch = dg(ctx_sc[half].reshape(rows, width), wo_ref[...], NN)
+    whole = x_sc[half].reshape(rows, width).astype(f32) + branch
+    unit, rs = norm_stats(whole)
+    normed[...] = (unit * gain + line(shift_ref)).astype(bf16)
 
     def enter(c, slot):
+        cols = cols_of(c)
+        v_sc[slot] = dg(normed[...], wi_ref[:, cols], NN) + bias_ref[cols].astype(f32).reshape(1, step)
+        g_sc[slot] = dg(y_sc[half].reshape(rows, width), wf_ref[cols, :], NT)
+
+    def leave(c, slot):
+        cols = cols_of(c)
+        v = v_sc[slot]
+        square = v * v
+        side = 0.5 * jnp.tanh(v * (c0 + c1 * square)) + 0.5
+        act = v * side
+        slope = side + act * (1.0 - side) * (2.0 * c0 + 6.0 * c1 * square)
+        feed_sc[...] += dg(act.astype(bf16), wf_ref[cols, :], NN)
+        grad_sc[...] += dg((slope * g_sc[slot]).astype(bf16), wi_ref[:, cols], NT)
+
+    def wait_weights(*which):
         @pl.when(first)
         def _():
-            load_i(c).wait()
-            load_f(c).wait()
-
-        cols = cols_of(c)
-        v_sc[slot] = dg(normed_sc[...], wi_ref[:, cols], NN) + bias_ref[cols].astype(f32).reshape(1, step)
-        g_sc[slot] = dg(y_ref[...].reshape(rows, width), wf_ref[cols, :], NT)
-
-    def leave(c, slot):
-        v = v_sc[slot]
-        square = v * v
-        half = 0.5 * jnp.tanh(v * (c0 + c1 * square)) + 0.5
-        act = v * half
-        slope = half + act * (1.0 - half) * (2.0 * c0 + 6.0 * c1 * square)
-        cols = cols_of(c)
-        feed_sc[...] += dg(act.astype(bf16), wf_ref[cols, :], NN)
-        grad_sc[...] += dg((slope * g_sc[slot]).astype(bf16), wi_ref[:, cols], NT)
+            for c in which:
+                load_i(c).wait()
+                load_f(c).wait()
+
+    @pl.when(first)
+    def _():
+        load_y(0).wait()
+        load_i(0).wait()
+        load_f(0).wait()
+
+    @pl.when(half == 1)
+    def _():
+        take_y().wait()
 
     feed_sc[...] = jnp.zeros_like(feed_sc)
     grad_sc[...] = jnp.zeros_like(grad_sc)
     enter(0, 0)
 
+    @pl.when(first)
+    def _():
+        entry_wait(1)
+        take_y().start()
+
     def pair(i, carry):
+        wait_weights(2 * i + 1, 2 * i + 2)
         enter(2 * i + 1, 1)
         leave(2 * i, 0)
         enter(2 * i + 2, 0)
@@ -771,68 +844,78 @@
         return carry
 
     lax.fori_loop(0, chunks // 2 - 1, pair, 0)
+    wait_weights(chunks - 1)
     enter(chunks - 1, 1)
     leave(chunks - 2, 0)
     leave(chunks - 1, 1)
     feed = feed_sc[...]
-    result = hidden + feed
-    out_ref[...] = result.astype(bf16).reshape(out_ref.shape)
-    valid = jnp.concatenate([column(mask_ref[b, 0:1, :])[:, 0:1] for b in range(blocks)], 0)
+    result = whole + feed
+    out_sc[half] = result.astype(bf16).reshape(out_sc.shape[1:])
+    valid = jnp.concatenate([column(mask_ref[base(half) + b, 0:1, :])[:, 0:1] for b in range(2)], 0)
     one = jnp.sum(valid * jnp.sum(result * result, axis=1, keepdims=True))
     two = jnp.sum(valid * jnp.sum(branch * branch + feed * feed, axis=1, keepdims=True))
     count = jnp.sum(valid)
     row = lax.broadcasted_iota(jnp.int32, sums_ref.shape, 0)
     col = lax.broadcasted_iota(jnp.int32, sums_ref.shape, 1)
-    mine = jnp.where(col == 0, one, jnp.where(col == 1, two, jnp.where(col == 2, count, 0.0)))
-    mine = jnp.where(row == 0, mine, 0.0)
+    total = jnp.where(col == 0, one, jnp.where(col == 1, two, jnp.where(col == 2, count, 0.0)))
+    sums_ref[...] += jnp.where(row == 0, total, 0.0)
+    dy = y_sc[half].reshape(rows, width).astype(f32)
+    low = (dy + norm_grad(unit, rs, gain, grad_sc[...])).astype(bf16)
+    hg_sc[half] = low.reshape(hg_sc.shape[1:])
+    cg_sc[half] = dg(low, wo_ref[...], NT).astype(bf16)
+
+    def saves(h):
+        flat = pl.ds(pl.multiple_of(base(h) * tile, tile), rows)
+        return [
+            pltpu.make_async_copy(out_sc.at[h], slabs(out_hbm, h), save_sem.at[h, 0]),
+            pltpu.make_async_copy(hg_sc.at[h], slabs(hg_hbm, h), save_sem.at[h, 1]),
+            pltpu.make_async_copy(cg_sc.at[h], cg_hbm.at[flat, :], save_sem.at[h, 2]),
+        ]
+
+    for copy in saves(half):
+        copy.start()
 
     @pl.when(first)
     def _():
-        sums_ref[...] = mine
-
-    @pl.when(jnp.logical_not(first))
-    def _():
-        sums_ref[...] += mine
-
-    dy = y_ref[...].reshape(rows, width).astype(f32)
-    low = (dy + norm_grad(unit, rs, gain, grad_sc[...])).astype(bf16)
-    hg_ref[...] = low
-    cg_ref[...] = dg(low, wo_ref[...], NT).astype(bf16)
-
-
-def feed(x, dy, context, mask, wo, gain, shift, wi, bias, wf):
+        load_y(1).wait()
+        load_ctx(1).wait()
+        load_x(1).wait()
+
+    @pl.when(half == 1)
+    def _():
+        for copy in saves(0) + saves(1):
+            copy.wait()
+
+
+def feed(x, y, dy, context, mask, wo, gain, shift, wi, bias, wf):
     slots, tile, width = x.shape
-    rows = slots * tile
+    rows = slots // 2 * tile
     units = wi.shape[1]
-    each = 2
     step = 512
-    slab = pl.BlockSpec((each, tile, width), lambda i: (i, 0, 0))
-    flat = pl.BlockSpec((each * tile, width), lambda i: (i, 0))
+    chunks = units // step
+    pair = (2, 2, tile, width)
+    dma = pltpu.SemaphoreType.DMA
     return pl.pallas_call(
         functools.partial(feed_kernel, step=step),
-        grid=(slots // each,),
-        in_specs=[
-            slab, slab, flat,
-            pl.BlockSpec((each,) + mask.shape[1:], lambda i: (i, 0, 0)),
-            ANY, ANY, ANY, resident(gain.shape), resident(shift.shape), resident(bias.shape),
+        grid=(2,),
+        in_specs=[ANY] * 7 + [resident(a.shape) for a in (mask, gain, shift, bias)],
+        out_specs=[ANY] * 3 + [pl.BlockSpec((8, width), lambda h: (0, 0))],
+        out_shape=[jax.ShapeDtypeStruct(x.shape, bf16)] * 2 + [
+            jax.ShapeDtypeStruct((2 * rows, width), bf16), jax.ShapeDtypeStruct((8, width), f32)
         ],
-        out_specs=[slab, flat, flat, pl.BlockSpec((8, width), lambda i: (0, 0))],
-        out_shape=[
-            jax.ShapeDtypeStruct(x.shape, bf16),
-            jax.ShapeDtypeStruct((rows, width), bf16),
-            jax.ShapeDtypeStruct((rows, width), bf16),
-            jax.ShapeDtypeStruct((8, width), f32),
+        scratch_shapes=[pltpu.VMEM(pair, bf16)] * 3 + [
+            pltpu.VMEM(wo.shape, bf16), pltpu.VMEM(wi.shape, bf16), pltpu.VMEM(wf.shape, bf16),
+            pltpu.VMEM((rows, width), bf16),
+            pltpu.VMEM((rows, width), f32), pltpu.VMEM((rows, width), f32),
+            pltpu.VMEM((2, rows, step), f32), pltpu.VMEM((2, rows, step), f32),
+            pltpu.VMEM(pair, bf16), pltpu.VMEM(pair, bf16), pltpu.VMEM((2, rows, width), bf16),
+            dma((2, 4)), dma((2, chunks)), dma((2, 3)), dma, dma,
         ],
-        scratch_shapes=[
-            pltpu.VMEM(wo.shape, bf16), pltpu.VMEM(wi.shape, bf16), pltpu.VMEM(wf.shape, bf16),
-            pltpu.VMEM((each * tile, width), f32), pltpu.VMEM((each * tile, width), f32),
-            pltpu.VMEM((each * tile, width), bf16),
-            pltpu.VMEM((2, each * tile, step), f32), pltpu.VMEM((2, each * tile, step), f32),
-            pltpu.SemaphoreType.DMA((2 * (units // step) + 1,)),
-        ],
-        compiler_params=params(62),
+        compiler_params=pltpu.CompilerParams(
+            collective_id=2, has_side_effects=True, vmem_limit_bytes=62 * MIB, dimension_semantics=("arbitrary",)
+        ),
         name="feed",
-    )(x, dy, context, mask, wo, wi, wf, gain, shift, bias)
+    )(x, y, dy, context.reshape(x.shape), wo, wi, wf, mask, gain, shift, bias)
 
 
 def close_kernel(
@@ -852,7 +935,7 @@
     heads = GROUP // size
     rank = downq_ref.shape[0]
     step = pl.program_id(0)
-    last = 2 * groups + 1
+    last = 2 * groups + 5
     group, me = lax.axis_index("dp"), lax.axis_index("head")
     mine = lax.rem(me, 2)
     near = me - mine
@@ -959,20 +1042,22 @@
             grads[a, far_rows, cols] = (loc[a, far_rows, :] * scales[a]).astype(bf16)
             near_sc[a, :, cols] = loc[a, near_rows, :]
 
-    @pl.when((step > groups) & (step < last))
-    def _():
-        cols = pl.ds(pl.multiple_of((step - groups - 1) * GROUP, GROUP), GROUP)
+    @pl.when((step > groups + 2) & (step < 2 * groups + 3))
+    def _():
+        cols = pl.ds(pl.multiple_of((step - groups - 3) * GROUP, GROUP), GROUP)
         near_rows = rows_at(near * tile, 0, half)
         attention(diag_units(near * tile))
         for a in range(3):
             both = loc[a, near_rows, :] + near_sc[a, :, cols]
             grads[a, near_rows, cols] = (both * scales[a]).astype(bf16)
 
+    held = tile // 4
+
     def give(k):
         return remote(res_sc.at[peers[k][1]], out_ref.at[me], send.at[k], recv.at[k], peers[k])
 
     def give_part(p):
-        rows = pl.ds(p * (tile // 2), tile // 2)
+        rows = pl.ds(0, tile - held) if p == 0 else pl.ds(tile - held, held)
         return remote(
             res_sc.at[peers[1][1], rows], out_ref.at[me, rows], send.at[1 + 2 * p], recv.at[1 + 2 * p], peers[1]
         )
@@ -997,13 +1082,12 @@
         for copy in loads():
             copy.wait()
 
-    @pl.when((step == groups) | (step == last))
-    def _():
-        first = far + (near - far) * lax.div(step, last)
-        at = pl.ds(first, 2)
+    @pl.when((step == groups + 2) | (step == 2 * groups + 3))
+    def _():
+        first = far + (near - far) * lax.div(step, 2 * groups + 3)
         here = pl.ds(pl.multiple_of(first * tile, tile), half)
-        dq, dk, dv = grads[0, here, :], grads[1, here, :], grads[2, here, :]
-        normed = normed_sc[at].reshape(half, width)
+        dq, dv = grads[0, here, :], grads[2, here, :]
+        normed = normed_sc[pl.ds(first, 2)].reshape(half, width)
         low_gq = (ADAPTER_SCALE * dg(dq, upq_ref[...], NT)).astype(bf16)
         low_gv = (ADAPTER_SCALE * dg(dv, upv_ref[...], NT)).astype(bf16)
         low_q = dg(normed, downq_ref[...], NT).astype(bf16)
@@ -1013,11 +1097,31 @@
         sums[2 * rank : 3 * rank] += ADAPTER_SCALE * dg(low_q, dq, TN)
         sums[3 * rank : 4 * rank] += ADAPTER_SCALE * dg(low_v, dv, TN)
 
-        @pl.when(step == last)
-        def _():
-            for k in range(len(rest)):
-                scatter(k).start()
-
+    @pl.when(step == 2 * groups + 3)
+    def _():
+        for k in range(len(rest)):
+            scatter(k).start()
+
+    @pl.when(step == last)
+    def _():
+        pair(0, peers[2]).wait()
+        chunk[1] = chunk[0] + heard[0]
+        pair(1, peers[0]).start()
+        give_part(1).start()
+
+    early = (step == groups) | (step == groups + 1)
+
+    @pl.when(early | (step > 2 * groups + 3))
+    def _():
+        late = lax.div(step, 2 * groups + 4)
+        second = lax.rem(step, 2)
+        slab = late * (beside + second * (me - beside)) + (1 - late) * (
+            peers[0][1] + second * (peers[1][1] - peers[0][1])
+        )
+        here = pl.ds(pl.multiple_of(slab * tile, tile), tile)
+        dq, dk, dv = grads[0, here, :], grads[1, here, :], grads[2, here, :]
+        low_gq = (ADAPTER_SCALE * dg(dq, upq_ref[...], NT)).astype(bf16)
+        low_gv = (ADAPTER_SCALE * dg(dv, upv_ref[...], NT)).astype(bf16)
         normed_grad = (
             dg(dq, w_sc[:, :width], NT)
             + dg(dk, w_sc[:, width : 2 * width], NT)
@@ -1025,19 +1129,21 @@
             + dg(low_gq, downq_ref[...], NN)
             + dg(low_gv, downv_ref[...], NN)
         )
-        unit, rs = norm_stats(x_sc[at].reshape(half, width).astype(f32))
-        grad = hg_sc[at].reshape(half, width).astype(f32) + norm_grad(unit, rs, line(gain_ref), normed_grad)
-        res_sc[at] = grad.astype(bf16).reshape(2, tile, width)
+        unit, rs = norm_stats(x_sc[slab].astype(f32))
+        grad = hg_sc[slab].astype(f32) + norm_grad(unit, rs, line(gain_ref), normed_grad)
+        res_sc[slab] = grad.astype(bf16)
 
     @pl.when(step == groups)
     def _():
         give(0).start()
+
+    @pl.when(step == groups + 1)
+    def _():
         give_part(0).start()
 
-    @pl.when(step == last)
+    @pl.when(step == 2 * groups + 4)
     def _():
         give(2).start()
-        keep().start()
         for k in range(len(rest)):
             scatter(k).wait()
         whole = sums[:, block_of(group)]
@@ -1045,10 +1151,10 @@
             whole = whole + parts[k]
         chunk[0] = whole
         pair(0, peers[2]).start()
-        pair(0, peers[2]).wait()
-        chunk[1] = chunk[0] + heard[0]
-        pair(1, peers[0]).start()
-        give_part(1).start()
+
+    @pl.when(step == last)
+    def _():
+        keep().start()
         pair(1, peers[0]).wait()
         whole = chunk[1] + heard[1]
         chunk[2] = whole
@@ -1088,8 +1194,8 @@
         return a.reshape(x.shape)
 
     def of(t):
-        second = lax.div(t, groups + 1)
-        return jnp.minimum(t - second * (groups + 1), groups - 1)
+        second = lax.div(t, groups + 3)
+        return jnp.minimum(t - second * (groups + 3), groups - 1)
 
     def early(t):
         return jnp.minimum(t, groups - 1)
@@ -1099,11 +1205,11 @@
 
     return pl.pallas_call(
         functools.partial(close_kernel, size=size, strip=32, sizes=sizes),
-        grid=(2 * groups + 2,),
+        grid=(2 * groups + 6,),
         in_specs=[
             columns(0), columns(1), columns(2), columns(0), columns(0), columns(0),
             pl.BlockSpec((half, GROUP), lambda t: (0, early(t))),
-            pl.BlockSpec((1, per, half, half), lambda t: (1 - lax.div(t, groups + 1), of(t), 0, 0)),
+            pl.BlockSpec((1, per, half, half), lambda t: (1 - jnp.minimum(lax.div(t, groups + 3), 1), of(t), 0, 0)),
             pl.BlockSpec((per, half, half), lambda t: (early(t), 0, 0)),
         ]
         + [ANY] * 5
@@ -1142,8 +1248,15 @@
     )(qkv, qkv, qkv, grad, context, cd, cc, pd, pc, result, x, fold(hidden_grad), fold(normed), w, *small)
 
 
-def finish_kernel(total_ref, aq_ref, bq_ref, av_ref, bv_ref, rms_ref):
+def finish_kernel(total_ref, a_hbm, b_hbm, aq_ref, bq_ref, av_ref, bv_ref, rms_ref, a_out, b_out, a_sc, b_sc, sem):
     rank, width = aq_ref.shape
+    loads, saves = [], []
+    for k, (src, kept, dst) in enumerate(((a_hbm, a_sc, a_out), (b_hbm, b_sc, b_out))):
+        for s in range(src.shape[0]):
+            loads.append(pltpu.make_async_copy(src.at[s], kept.at[s], sem.at[k, s, 0]))
+            saves.append(pltpu.make_async_copy(kept.at[s], dst.at[s], sem.at[k, s, 1]))
+    for load in loads:
+        load.start()
     aq_ref[...] = total_ref[0:rank]
     av_ref[...] = total_ref[rank : 2 * rank]
     bq_ref[...] = total_ref[2 * rank : 3 * rank]
@@ -1151,19 +1264,33 @@
     line = total_ref[4 * rank : 4 * rank + 1, 0:128]
     lane = lax.broadcasted_iota(jnp.int32, line.shape, 1)
     count = jnp.maximum(jnp.sum(jnp.where(lane == 2, line, 0.0)), 1.0)
-    rms_ref[...] = jnp.sqrt(line / (jnp.where(lane == 0, 1.0, 2.0) * count * width))
-
-
-def finish(total, rank):
+    values = jnp.sqrt(line / (jnp.where(lane == 0, 1.0, 2.0) * count * width))
+    for k in range(2):
+        rms_ref[k] = jnp.sum(jnp.where(lane == k, values, 0.0))
+    for load, save in zip(loads, saves):
+        load.wait()
+        save.start()
+    for save in saves:
+        save.wait()
+
+
+def finish(total, a, b, rank):
     width = total.shape[1]
     small = jax.ShapeDtypeStruct((rank, width), f32)
     return pl.pallas_call(
         finish_kernel,
-        in_specs=[VMEM],
-        out_specs=[VMEM] * 5,
-        out_shape=[small] * 4 + [jax.ShapeDtypeStruct((1, 128), f32)],
+        in_specs=[VMEM, ANY, ANY],
+        out_specs=[VMEM] * 4 + [pl.BlockSpec(memory_space=pltpu.SMEM), ANY, ANY],
+        out_shape=[small] * 4 + [
+            jax.ShapeDtypeStruct((2,), f32),
+            jax.ShapeDtypeStruct(a.shape, a.dtype),
+            jax.ShapeDtypeStruct(b.shape, b.dtype),
+        ],
+        scratch_shapes=[
+            pltpu.VMEM(a.shape, a.dtype), pltpu.VMEM(b.shape, b.dtype), pltpu.SemaphoreType.DMA((2, a.shape[0], 2))
+        ],
         name="finish",
-    )(total)
+    )(total, a, b)
 
 
 def whole_slots(
@@ -1195,15 +1322,15 @@
         first_norm_gain, first_norm_bias, downq, downv, query_up_weight, value_up_weight, size,
     )
     out, hidden_grad, context_grad, sums = feed(
-        x, dy, context, mask, attention_out_weight, second_norm_gain, second_norm_bias,
+        x, dy, output_gradient, context, mask, attention_out_weight, second_norm_gain, second_norm_bias,
         feed_input_weight, feed_input_bias, feed_output_weight,
     )
     output, input_grad, total = closing(
         qkv, context_grad, context, cd, cc, pd, pc, out, x, hidden_grad, normed, query_key_value_weight,
         first_norm_gain, downq, downv, query_up_weight, value_up_weight, sums, size, sizes,
     )
-    grad_aq, grad_bq, grad_av, grad_bv, rms = finish(total, rank)
-    return output, input_grad, grad_aq.T, grad_bq, grad_av.T, grad_bv, rms[0, :2]
+    grad_aq, grad_bq, grad_av, grad_bv, rms, output, input_grad = finish(total, output, input_grad, rank)
+    return output, input_grad, grad_aq.T, grad_bq, grad_av.T, grad_bv, rms
 
 
 def body(*args):

time: 180 us -> 177 us (0.983)
  local copies, waits for them, and re-layouts: 5.72 us -> 0 us
  Pallas kernels: 173 us -> 175 us
    pallas_call x2, Pallas kernels: 55.7 us -> 61.5 us  [the longest x1 56.4 us: feed(): pl.pallas_call(functools.partial(feed_kernel, step=step), grid=(2,), in_s...]
    pallas_call x1, Pallas kernels: 56 us -> 50.6 us  [opening(): pl.pallas_call(functools.partial(open_kernel, size=size, strip=32), grid=...]
    unnamed x4 -> x0, local copies, waits for them, and re-layouts: 4.55 us -> none
where the time goes in v2:
time: 177 us; the launch traced here: 176 us
  Pallas kernels  175 us (99%)
    pallas_call x1, Pallas kernels, closing(): pl.pallas_call(functools.partial(close_kernel, size=size, strip=32, sizes...  63.2 us
    pallas_call x1, Pallas kernels, feed(): pl.pallas_call(functools.partial(feed_kernel, step=step), grid=(2,), in_s...  56.4 us
    pallas_call x1, Pallas kernels, opening(): pl.pallas_call(functools.partial(open_kernel, size=size, strip=32), grid=...  50.6 us
    pallas_call x1, Pallas kernels, finish(): pl.pallas_call(finish_kernel, in_specs=[VMEM, ANY, ANY], out_specs=[VMEM]...  5.14 us

profile of v2, /device:TPU:0, one launch (start us, length us, event | category | flops | bytes accessed | tf_op | source)
XLA Modules:
  0.0 176.2 jit_solution(14573532567439241170)
XLA Ops:
  0.6 50.6 %opening.1 = (bf16[4,256,1024]{2,1,0:T(8,128)(2,1)}, bf16[4,256,1024]{2,1,0:T(8,128)(2,1)}, f32[4,8,256]{2,1,0:T(8,128)}, bf16[1024,1024]{1,0:T(8,128)(2,1)}, bf...) custom-call(bf16[4,256,1024]{2,1,0:T(8,128)(2,1)} %x_ref.1, ...), custom_call_target="tpu_custom_call" | custom-call | tf_op jit(solution)/shard_map/opening/pallas_call | solution.py:673
  51.2 56.4 %feed.1 = (bf16[4,256,1024]{2,1,0:T(8,128)(2,1)}, bf16[4,256,1024]{2,1,0:T(8,128)(2,1)}, bf16[1024,1024]{1,0:T(8,128)(2,1)}, f32[8,1024]{1,0:T(8,128)}) custom-call(bf16[4,256,1024]{2,1,0:T(8,128)(2,1)} %get-tuple-element.32.x_hbm, bf16[4,256,1024]{2,1,0:T(8,128)(2,1)} %get-tuple-element.33.y_hbm, bf16[4,256,1024]{2,1,0:T(8,128)(2,1)} %dy_hbm.1, ...), custom_call_target="tpu_custom_call" | custom-call | tf_op jit(solution)/shard_map/feed/pallas_call | solution.py:898
  107.6 63.2 %closing.1 = (bf16[4,256,1024]{2,1,0:T(8,128)(2,1)}, bf16[4,256,1024]{2,1,0:T(8,128)(2,1)}, f32[24,1024]{1,0:T(8,128)}) custom-call(bf16[1024,3072]{1,0:T(8,128)(2,1)} %get-tuple-element.31.q_ref.k_ref.v_ref, bf16[1024,3072]{1,0:T(8,128)(2,1)} %get-tuple-element.31.q_ref.k_ref.v_ref, bf16[1024,3072]{1,0:T(8,128)(2,1)} %get-tuple-element.31.q_ref.k_ref.v_ref, ...), custom_call_target="tpu_custom_call" | custom-call | tf_op jit(solution)/shard_map/closing/pallas_call | solution.py:1206
  170.9 5.1 %finish.1 = (f32[4,1024]{1,0:T(4,128)}, f32[4,1024]{1,0:T(4,128)}, f32[4,1024]{1,0:T(4,128)}, f32[4,1024]{1,0:T(4,128)}, f32[2]{0:T(128)}, /*index=5*/bf16[4,256,1024]{2,1,0:T(8,128)(2,1)}, bf16[4,256,1024]{2,1,0:T(8,128)(2,1)}) custom-call(f32[24,1024]{1,0:T(8,128)} %get-tuple-element.45.total_ref, bf16[4,256,1024]{2,1,0:T(8,128)(2,1)} %get-tuple-element.46.a_hbm, ...), custom_call_target="tpu_custom_call" | custom-call | tf_op jit(solution)/shard_map/finish/pallas_call | solution.py:1280

commit v3 on v2

--- a/solution.py
+++ b/solution.py
@@ -425,8 +425,8 @@
 
 def open_kernel(
     x_ref, dy_ref, w_ref, mask_ref, start_ref, gain_ref, shift_ref, downq_ref, downv_ref, upq_ref, upv_ref,
-    xs_ref, dys_ref, masks_ref, normed_ref, qkv_ref, ctx_ref, pd_ref, pc_ref, cd_ref, cc_ref,
-    x_sc, y_sc, w_sc, mask_sc, normed_sc, qkv_sc, s_sc, diag_sc, cross_sc, first_sc, near_sc, state, part,
+    xs_ref, dys_ref, masks_ref, normed_ref, low_ref, qkv_ref, ctx_ref, pd_ref, pc_ref, cd_ref, cc_ref,
+    x_sc, y_sc, w_sc, mask_sc, normed_sc, low_sc, qkv_sc, s_sc, diag_sc, cross_sc, first_sc, near_sc, state, part,
     x_send, x_recv, y_send, y_recv, m_send, m_recv, local_sem,
     *, size, strip,
 ):
@@ -476,6 +476,9 @@
     def save_normed():
         return pltpu.make_async_copy(normed_sc, normed_ref, local_sem.at[5])
 
+    def save_low():
+        return pltpu.make_async_copy(low_sc, low_ref, local_sem.at[8])
+
     def save_qkv():
         return pltpu.make_async_copy(qkv_sc, qkv_ref, local_sem.at[6])
 
@@ -538,6 +541,8 @@
         normed_sc[here, :] = normed
         low_q = dg(normed, downq_ref[...], NT).astype(bf16)
         low_v = dg(normed, downv_ref[...], NT).astype(bf16)
+        low_sc[0, here, :] = low_q
+        low_sc[1, here, :] = low_v
         scale = size**-0.5 * LOG2E
         wide = 512
         for at in range(0, 3 * width, wide):
@@ -552,6 +557,7 @@
     @pl.when(step == middle)
     def _():
         save_normed().start()
+        save_low().start()
         save_qkv().start()
 
     def attention(g, units):
@@ -648,6 +654,7 @@
         save_x().wait()
         save_y().wait()
         save_normed().wait()
+        save_low().wait()
         save_qkv().wait()
 
 
@@ -674,7 +681,7 @@
         functools.partial(open_kernel, size=size, strip=32),
         grid=(middle + groups + 1,),
         in_specs=[ANY] * 3 + [resident(a.shape) for a in small],
-        out_specs=[ANY] * 5 + [
+        out_specs=[ANY] * 6 + [
             pl.BlockSpec((length, GROUP), lambda t: (0, late(t))),
             pl.BlockSpec((1, per, half, half), diag_at),
             pl.BlockSpec((per, half, half), lambda t: (late(t), 0, 0)),
@@ -686,6 +693,7 @@
             jax.ShapeDtypeStruct(x.shape, bf16),
             jax.ShapeDtypeStruct(masks, f32),
             jax.ShapeDtypeStruct((length, width), bf16),
+            jax.ShapeDtypeStruct((2, length, downq.shape[0]), bf16),
             jax.ShapeDtypeStruct((length, 3 * width), bf16),
             jax.ShapeDtypeStruct((length, width), bf16),
             jax.ShapeDtypeStruct((2, per * groups, half, half), bf16),
@@ -699,6 +707,7 @@
             pltpu.VMEM(w.shape, bf16),
             pltpu.VMEM(masks, f32),
             pltpu.VMEM((length, width), bf16),
+            pltpu.VMEM((2, length, downq.shape[0]), bf16),
             pltpu.VMEM((length, 3 * width), bf16),
             pltpu.VMEM((2, per * TILE, half), f32),
             pltpu.VMEM((length, half), f32),
@@ -707,7 +716,7 @@
             pltpu.VMEM((3, half, width), f32),
             pltpu.VMEM((3, length, GROUP), f32),
             pltpu.VMEM((3, half, GROUP), f32),
-            dma((3,)), dma((3,)), dma((3,)), dma((3,)), dma((3,)), dma((3,)), dma((8,)),
+            dma((3,)), dma((3,)), dma((3,)), dma((3,)), dma((3,)), dma((3,)), dma((9,)),
         ],
         compiler_params=pltpu.CompilerParams(
             collective_id=0, has_side_effects=True, vmem_limit_bytes=62 * MIB, dimension_semantics=("arbitrary",)
@@ -761,11 +770,14 @@
     def cols_of(c):
         return pl.ds(c * step if isinstance(c, int) else pl.multiple_of(c * step, step), step)
 
+    def twice(c):
+        return pl.ds(2 * c * step if isinstance(c, int) else pl.multiple_of(2 * c * step, 2 * step), 2 * step)
+
     def load_i(c):
-        return pltpu.make_async_copy(wi_hbm.at[:, cols_of(c)], wi_ref.at[:, cols_of(c)], chunk_sem.at[0, c])
+        return pltpu.make_async_copy(wi_hbm.at[:, twice(c)], wi_ref.at[:, twice(c)], chunk_sem.at[0, c])
 
     def load_f(c):
-        return pltpu.make_async_copy(wf_hbm.at[cols_of(c), :], wf_ref.at[cols_of(c), :], chunk_sem.at[1, c])
+        return pltpu.make_async_copy(wf_hbm.at[twice(c), :], wf_ref.at[twice(c), :], chunk_sem.at[1, c])
 
     @pl.when(first)
     def _():
@@ -773,14 +785,13 @@
         load_o().start()
         load_ctx(0).start()
         load_x(0).start()
-        for c in range(chunks):
+        load_y(0).start()
+        for c in range(chunks // 2):
             load_i(c).start()
             load_f(c).start()
-            if c == 1:
-                load_y(0).start()
-                load_y(1).start()
-                load_ctx(1).start()
-                load_x(1).start()
+        load_y(1).start()
+        load_ctx(1).start()
+        load_x(1).start()
         sums_ref[...] = jnp.zeros_like(sums_ref)
         load_o().wait()
         load_ctx(0).wait()
@@ -809,12 +820,11 @@
         feed_sc[...] += dg(act.astype(bf16), wf_ref[cols, :], NN)
         grad_sc[...] += dg((slope * g_sc[slot]).astype(bf16), wi_ref[:, cols], NT)
 
-    def wait_weights(*which):
+    def wait_weights(c):
         @pl.when(first)
         def _():
-            for c in which:
-                load_i(c).wait()
-                load_f(c).wait()
+            load_i(c).wait()
+            load_f(c).wait()
 
     @pl.when(first)
     def _():
@@ -836,7 +846,7 @@
         take_y().start()
 
     def pair(i, carry):
-        wait_weights(2 * i + 1, 2 * i + 2)
+        wait_weights(i + 1)
         enter(2 * i + 1, 1)
         leave(2 * i, 0)
         enter(2 * i + 2, 0)
@@ -844,7 +854,6 @@
         return carry
 
     lax.fori_loop(0, chunks // 2 - 1, pair, 0)
-    wait_weights(chunks - 1)
     enter(chunks - 1, 1)
     leave(chunks - 2, 0)
     leave(chunks - 1, 1)
@@ -909,7 +918,7 @@
             pltpu.VMEM((rows, width), f32), pltpu.VMEM((rows, width), f32),
             pltpu.VMEM((2, rows, step), f32), pltpu.VMEM((2, rows, step), f32),
             pltpu.VMEM(pair, bf16), pltpu.VMEM(pair, bf16), pltpu.VMEM((2, rows, width), bf16),
-            dma((2, 4)), dma((2, chunks)), dma((2, 3)), dma, dma,
+            dma((2, 4)), dma((2, chunks // 2)), dma((2, 3)), dma, dma,
         ],
         compiler_params=pltpu.CompilerParams(
             collective_id=2, has_side_effects=True, vmem_limit_bytes=62 * MIB, dimension_semantics=("arbitrary",)
@@ -920,10 +929,10 @@
 
 def close_kernel(
     q_ref, k_ref, v_ref, g_ref, o_ref, cd_ref, cc_ref, pd_ref, pc_ref,
-    res_hbm, x_hbm, hg_hbm, normed_hbm, w_hbm,
+    res_hbm, x_hbm, hg_hbm, normed_hbm, w_hbm, low_hbm,
     gain_ref, downq_ref, downv_ref, upq_ref, upv_ref, sums_ref,
     result_ref, out_ref, total_ref,
-    dp_sc, ds_sc, inner_sc, do_sc, loc, near_sc, grads, x_sc, hg_sc, normed_sc, w_sc, res_sc,
+    dp_sc, ds_sc, inner_sc, ones_sc, do_sc, loc, near_sc, grads, x_sc, hg_sc, normed_sc, w_sc, low_sc, res_sc,
     sums, parts, chunk, heard, total_sc,
     r_send, r_recv, send, recv, local_sem, part_send, part_recv, pair_send, pair_recv, mean_send, mean_recv,
     *, size, strip, sizes,
@@ -954,7 +963,9 @@
     def loads():
         return [
             pltpu.make_async_copy(src, dst, local_sem.at[1 + a])
-            for a, (src, dst) in enumerate([(x_hbm, x_sc), (hg_hbm, hg_sc), (normed_hbm, normed_sc), (w_hbm, w_sc)])
+            for a, (src, dst) in enumerate(
+                [(x_hbm, x_sc), (hg_hbm, hg_sc), (normed_hbm, normed_sc), (w_hbm, w_sc), (low_hbm, low_sc.at[0:2])]
+            )
         ]
 
     @pl.when(step == 0)
@@ -965,6 +976,9 @@
             copy.start()
         sums[...] = jnp.zeros_like(sums)
         sums[4 * rank :, :] = sums_ref[...]
+        lane_head = lax.div(lax.broadcasted_iota(jnp.int32, ones_sc.shape, 0), size)
+        spot_head = lax.div(lax.broadcasted_iota(jnp.int32, ones_sc.shape, 1), 128)
+        ones_sc[...] = jnp.where(lane_head == spot_head, 1.0, 0.0).astype(bf16)
 
     @pl.when(step == 1)
     def _():
@@ -983,14 +997,15 @@
             for j in range(0, n, TILE):
                 dp_sc[at % 2, :, j : j + TILE] = dg(masked, v_ref[rows_at(k_base, j, TILE), :], NT)
             both = (grad.astype(f32) * o_ref[rows_at(q_base, i * TILE, TILE), :].astype(f32)).astype(bf16)
-            inner_sc[at % 2] = dg(stack(both), jnp.ones((GROUP, 128), bf16), NN)
+            inner_sc[at % 2] = dg(both, ones_sc[...], NN)
 
         def score_grads(at, unit):
             i, n, _, _, probs = unit[:5]
             for h in range(heads):
                 for r in range(0, TILE, strip):
                     here = h * TILE + r
-                    inner = jnp.concatenate([inner_sc[at % 2, here : here + strip, :]] * (n // 128), 1)
+                    inner = inner_sc[at % 2, r : r + strip, 128 * h : 128 * (h + 1)]
+                    inner = jnp.concatenate([inner] * (n // 128), 1)
                     prob = probs[h, i * TILE + r : i * TILE + r + strip, 0:n].astype(f32)
                     ds = prob * (dp_sc[at % 2, here : here + strip, 0:n] - inner)
                     ds_sc[at % 2, here : here + strip, 0:n] = ds.astype(bf16)
@@ -1063,7 +1078,7 @@
         )
 
     def keep():
-        return pltpu.make_async_copy(res_sc.at[me], out_ref.at[me], local_sem.at[5])
+        return pltpu.make_async_copy(res_sc.at[me], out_ref.at[me], local_sem.at[6])
 
     def block_of(d):
         return pl.ds(pl.multiple_of(d * lanes, lanes), lanes)
@@ -1081,6 +1096,13 @@
     def _():
         for copy in loads():
             copy.wait()
+
+    @pl.when((step == groups) | (step == 2 * groups + 3))
+    def _():
+        first = far + (near - far) * lax.div(step, 2 * groups + 3)
+        here = pl.ds(pl.multiple_of(first * tile, tile), half)
+        low_sc[2, here, :] = (ADAPTER_SCALE * dg(grads[0, here, :], upq_ref[...], NT)).astype(bf16)
+        low_sc[3, here, :] = (ADAPTER_SCALE * dg(grads[2, here, :], upv_ref[...], NT)).astype(bf16)
 
     @pl.when((step == groups + 2) | (step == 2 * groups + 3))
     def _():
@@ -1088,10 +1110,7 @@
         here = pl.ds(pl.multiple_of(first * tile, tile), half)
         dq, dv = grads[0, here, :], grads[2, here, :]
         normed = normed_sc[pl.ds(first, 2)].reshape(half, width)
-        low_gq = (ADAPTER_SCALE * dg(dq, upq_ref[...], NT)).astype(bf16)
-        low_gv = (ADAPTER_SCALE * dg(dv, upv_ref[...], NT)).astype(bf16)
-        low_q = dg(normed, downq_ref[...], NT).astype(bf16)
-        low_v = dg(normed, downv_ref[...], NT).astype(bf16)
+        low_q, low_v, low_gq, low_gv = (low_sc[a, here, :] for a in range(4))
         sums[0:rank] += dg(low_gq, normed, TN)
         sums[rank : 2 * rank] += dg(low_gv, normed, TN)
         sums[2 * rank : 3 * rank] += ADAPTER_SCALE * dg(low_q, dq, TN)
@@ -1120,8 +1139,7 @@
         )
         here = pl.ds(pl.multiple_of(slab * tile, tile), tile)
         dq, dk, dv = grads[0, here, :], grads[1, here, :], grads[2, here, :]
-        low_gq = (ADAPTER_SCALE * dg(dq, upq_ref[...], NT)).astype(bf16)
-        low_gv = (ADAPTER_SCALE * dg(dv, upv_ref[...], NT)).astype(bf16)
+        low_gq, low_gv = low_sc[2, here, :], low_sc[3, here, :]
         normed_grad = (
             dg(dq, w_sc[:, :width], NT)
             + dg(dk, w_sc[:, width : 2 * width], NT)
@@ -1175,7 +1193,7 @@
 
 
 def closing(
-    qkv, grad, context, cd, cc, pd, pc, result, x, hidden_grad, normed, w,
+    qkv, grad, context, cd, cc, pd, pc, result, x, hidden_grad, normed, w, low,
     gain, downq, downv, upq, upv, sums, size, sizes,
 ):
     slots, tile, width = x.shape
@@ -1212,7 +1230,7 @@
             pl.BlockSpec((1, per, half, half), lambda t: (1 - jnp.minimum(lax.div(t, groups + 3), 1), of(t), 0, 0)),
             pl.BlockSpec((per, half, half), lambda t: (early(t), 0, 0)),
         ]
-        + [ANY] * 5
+        + [ANY] * 6
         + [resident(a.shape) for a in small],
         out_specs=[ANY, ANY, pl.BlockSpec(total, lambda t: (0, 0))],
         out_shape=[
@@ -1223,7 +1241,8 @@
         scratch_shapes=[
             pltpu.VMEM((2, per * TILE, half), f32),
             pltpu.VMEM((2, per * TILE, half), bf16),
-            pltpu.VMEM((2, per * TILE, 128), f32),
+            pltpu.VMEM((2, TILE, per * 128), f32),
+            pltpu.VMEM((GROUP, per * 128), bf16),
             pltpu.VMEM((2, half, GROUP), bf16),
             pltpu.VMEM((3, length, GROUP), f32),
             pltpu.VMEM((3, half, width), f32),
@@ -1232,20 +1251,21 @@
             pltpu.VMEM(x.shape, bf16),
             pltpu.VMEM(x.shape, bf16),
             pltpu.VMEM(w.shape, bf16),
+            pltpu.VMEM((4, length, rank), bf16),
             pltpu.VMEM(x.shape, bf16),
             pltpu.VMEM(total, f32),
             pltpu.VMEM((rest, total[0], lanes), f32),
             pltpu.VMEM((3, total[0], lanes), f32),
             pltpu.VMEM((2, total[0], lanes), f32),
             pltpu.VMEM(total, f32),
-            dma((3,)), dma((3,)), dma((4,)), dma((4,)), dma((6,)),
+            dma((3,)), dma((3,)), dma((4,)), dma((4,)), dma((7,)),
             dma((rest,)), dma((rest,)), dma((2,)), dma((2,)), dma((rest,)), dma((rest,)),
         ],
         compiler_params=pltpu.CompilerParams(
             collective_id=1, has_side_effects=True, vmem_limit_bytes=62 * MIB, dimension_semantics=("arbitrary",)
         ),
         name="closing",
-    )(qkv, qkv, qkv, grad, context, cd, cc, pd, pc, result, x, fold(hidden_grad), fold(normed), w, *small)
+    )(qkv, qkv, qkv, grad, context, cd, cc, pd, pc, result, x, fold(hidden_grad), fold(normed), w, low, *small)
 
 
 def finish_kernel(total_ref, a_hbm, b_hbm, aq_ref, bq_ref, av_ref, bv_ref, rms_ref, a_out, b_out, a_sc, b_sc, sem):
@@ -1317,7 +1337,7 @@
     rank = query_down_weight.shape[1]
     downq = query_down_weight.T
     downv = value_down_weight.T
-    x, dy, mask, normed, qkv, context, pd, pc, cd, cc = opening(
+    x, dy, mask, normed, low, qkv, context, pd, pc, cd, cc = opening(
         block_input_rows, output_gradient, query_key_value_weight, counted_mask, document_starts,
         first_norm_gain, first_norm_bias, downq, downv, query_up_weight, value_up_weight, size,
     )
@@ -1326,7 +1346,7 @@
         feed_input_weight, feed_input_bias, feed_output_weight,
     )
     output, input_grad, total = closing(
-        qkv, context_grad, context, cd, cc, pd, pc, out, x, hidden_grad, normed, query_key_value_weight,
+        qkv, context_grad, context, cd, cc, pd, pc, out, x, hidden_grad, normed, query_key_value_weight, low,
         first_norm_gain, downq, downv, query_up_weight, value_up_weight, sums, size, sizes,
     )
     grad_aq, grad_bq, grad_av, grad_bv, rms, output, input_grad = finish(total, output, input_grad, rank)

time: 177 us -> 175 us (0.989)
  no operation moved by 1% of the time
where the time goes in v3:
time: 175 us
  Pallas kernels  174 us (99%)
    pallas_call x1, Pallas kernels, closing(): pl.pallas_call(functools.partial(close_kernel, size=size, strip=32, sizes...  63.1 us
    pallas_call x1, Pallas kernels, feed(): pl.pallas_call(functools.partial(feed_kernel, step=step), grid=(2,), in_s...  54.7 us
    pallas_call x1, Pallas kernels, opening(): pl.pallas_call(functools.partial(open_kernel, size=size, strip=32), grid=...  50.7 us
    pallas_call x1, Pallas kernels, finish(): pl.pallas_call(finish_kernel, in_specs=[VMEM, ANY, ANY], out_specs=[VMEM]...  5.14 us

profile of v3, /device:TPU:0, one launch (start us, length us, event | category | flops | bytes accessed | tf_op | source)
XLA Modules:
  0.0 174.5 jit_solution(10731585775429058279)
XLA Ops:
  0.6 50.7 %opening.1 = (bf16[4,256,1024]{2,1,0:T(8,128)(2,1)}, bf16[4,256,1024]{2,1,0:T(8,128)(2,1)}, f32[4,8,256]{2,1,0:T(8,128)}, bf16[1024,1024]{1,0:T(8,128)(2,1)}, bf...) custom-call(bf16[4,256,1024]{2,1,0:T(8,128)(2,1)} %x_ref.1, ...), custom_call_target="tpu_custom_call" | custom-call | tf_op jit(solution)/shard_map/opening/pallas_call | solution.py:680
  51.4 54.7 %feed.1 = (bf16[4,256,1024]{2,1,0:T(8,128)(2,1)}, bf16[4,256,1024]{2,1,0:T(8,128)(2,1)}, bf16[1024,1024]{1,0:T(8,128)(2,1)}, f32[8,1024]{1,0:T(8,128)}) custom-call(bf16[4,256,1024]{2,1,0:T(8,128)(2,1)} %get-tuple-element.33.x_hbm, bf16[4,256,1024]{2,1,0:T(8,128)(2,1)} %get-tuple-element.34.y_hbm, bf16[4,256,1024]{2,1,0:T(8,128)(2,1)} %dy_hbm.1, ...), custom_call_target="tpu_custom_call" | custom-call | tf_op jit(solution)/shard_map/feed/pallas_call | solution.py:907
  106.1 63.1 %closing.1 = (bf16[4,256,1024]{2,1,0:T(8,128)(2,1)}, bf16[4,256,1024]{2,1,0:T(8,128)(2,1)}, f32[24,1024]{1,0:T(8,128)}) custom-call(bf16[1024,3072]{1,0:T(8,128)(2,1)} %get-tuple-element.32.q_ref.k_ref.v_ref, bf16[1024,3072]{1,0:T(8,128)(2,1)} %get-tuple-element.32.q_ref.k_ref.v_ref, bf16[1024,3072]{1,0:T(8,128)(2,1)} %get-tuple-element.32.q_ref.k_ref.v_ref, ...), custom_call_target="tpu_custom_call" | custom-call | tf_op jit(solution)/shard_map/closing/pallas_call | solution.py:1224
  169.2 5.1 %finish.1 = (f32[4,1024]{1,0:T(4,128)}, f32[4,1024]{1,0:T(4,128)}, f32[4,1024]{1,0:T(4,128)}, f32[4,1024]{1,0:T(4,128)}, f32[2]{0:T(128)}, /*index=5*/bf16[4,256,1024]{2,1,0:T(8,128)(2,1)}, bf16[4,256,1024]{2,1,0:T(8,128)(2,1)}) custom-call(f32[24,1024]{1,0:T(8,128)} %get-tuple-element.47.total_ref, bf16[4,256,1024]{2,1,0:T(8,128)(2,1)} %get-tuple-element.48.a_hbm, ...), custom_call_target="tpu_custom_call" | custom-call | tf_op jit(solution)/shard_map/finish/pallas_call | solution.py:1300

commit v4 on v3

--- a/solution.py
+++ b/solution.py
@@ -317,7 +317,6 @@
 
 
 LOG2E = 1.4426950408889634
-LN2 = 0.6931471805599453
 TILE = 256
 GROUP = 256
 bf16 = jnp.bfloat16
@@ -543,7 +542,7 @@
         low_v = dg(normed, downv_ref[...], NT).astype(bf16)
         low_sc[0, here, :] = low_q
         low_sc[1, here, :] = low_v
-        scale = size**-0.5 * LOG2E
+        scale = size**-0.5
         wide = 512
         for at in range(0, 3 * width, wide):
             cols = slice(at, at + wide)
@@ -580,7 +579,7 @@
                 sums.append([])
                 for h in range(heads):
                     here = h * TILE + r
-                    s = s_sc[at % 2, here : here + strip, 0:n] + bias(i * TILE + r, n)
+                    s = s_sc[at % 2, here : here + strip, 0:n] * LOG2E + bias(i * TILE + r, n)
                     top = jnp.max(s, axis=1, keepdims=True)
                     e = jnp.exp2(s - top)
                     tops[-1].append(top)
@@ -996,8 +995,10 @@
             masked = stack(grad)
             for j in range(0, n, TILE):
                 dp_sc[at % 2, :, j : j + TILE] = dg(masked, v_ref[rows_at(k_base, j, TILE), :], NT)
-            both = (grad.astype(f32) * o_ref[rows_at(q_base, i * TILE, TILE), :].astype(f32)).astype(bf16)
-            inner_sc[at % 2] = dg(both, ones_sc[...], NN)
+            both = grad.astype(f32) * o_ref[rows_at(q_base, i * TILE, TILE), :].astype(f32)
+            high = both.astype(bf16)
+            rest_of = (both - high.astype(f32)).astype(bf16)
+            inner_sc[at % 2] = dg(high, ones_sc[...], NN) + dg(rest_of, ones_sc[...], NN)
 
         def score_grads(at, unit):
             i, n, _, _, probs = unit[:5]
@@ -1043,7 +1044,7 @@
         do_sc[1] = (g_ref[half:, :].astype(f32) * cc_ref[...]).astype(bf16)
         return [(i, half, half, 0, pc_ref, 1, 0, True) for i in range(half // TILE)]
 
-    scales = (size**-0.5, LN2, 1.0)
+    scales = (size**-0.5, 1.0, 1.0)
 
     @pl.when(step < groups)
     def _():

time: 175 us -> 175 us (level)
  no operation moved by 1% of the time
where the time goes in v4:
time: 175 us
  Pallas kernels  174 us (99%)
    pallas_call x1, Pallas kernels, closing(): pl.pallas_call(functools.partial(close_kernel, size=size, strip=32, sizes...  63.3 us
    pallas_call x1, Pallas kernels, feed(): pl.pallas_call(functools.partial(feed_kernel, step=step), grid=(2,), in_s...  54.7 us
    pallas_call x1, Pallas kernels, opening(): pl.pallas_call(functools.partial(open_kernel, size=size, strip=32), grid=...  50.7 us
    pallas_call x1, Pallas kernels, finish(): pl.pallas_call(finish_kernel, in_specs=[VMEM, ANY, ANY], out_specs=[VMEM]...  5.14 us

profile of v4, /device:TPU:0, one launch (start us, length us, event | category | flops | bytes accessed | tf_op | source)
XLA Modules:
  0.0 174.7 jit_solution(8585428937150995957)
XLA Ops:
  0.6 50.7 %opening.1 = (bf16[4,256,1024]{2,1,0:T(8,128)(2,1)}, bf16[4,256,1024]{2,1,0:T(8,128)(2,1)}, f32[4,8,256]{2,1,0:T(8,128)}, bf16[1024,1024]{1,0:T(8,128)(2,1)}, bf...) custom-call(bf16[4,256,1024]{2,1,0:T(8,128)(2,1)} %x_ref.1, ...), custom_call_target="tpu_custom_call" | custom-call | tf_op jit(solution)/shard_map/opening/pallas_call | solution.py:679
  51.3 54.7 %feed.1 = (bf16[4,256,1024]{2,1,0:T(8,128)(2,1)}, bf16[4,256,1024]{2,1,0:T(8,128)(2,1)}, bf16[1024,1024]{1,0:T(8,128)(2,1)}, f32[8,1024]{1,0:T(8,128)}) custom-call(bf16[4,256,1024]{2,1,0:T(8,128)(2,1)} %get-tuple-element.33.x_hbm, bf16[4,256,1024]{2,1,0:T(8,128)(2,1)} %get-tuple-element.34.y_hbm, bf16[4,256,1024]{2,1,0:T(8,128)(2,1)} %dy_hbm.1, ...), custom_call_target="tpu_custom_call" | custom-call | tf_op jit(solution)/shard_map/feed/pallas_call | solution.py:906
  106.0 63.3 %closing.1 = (bf16[4,256,1024]{2,1,0:T(8,128)(2,1)}, bf16[4,256,1024]{2,1,0:T(8,128)(2,1)}, f32[24,1024]{1,0:T(8,128)}) custom-call(bf16[1024,3072]{1,0:T(8,128)(2,1)} %get-tuple-element.32.q_ref.k_ref.v_ref, bf16[1024,3072]{1,0:T(8,128)(2,1)} %get-tuple-element.32.q_ref.k_ref.v_ref, bf16[1024,3072]{1,0:T(8,128)(2,1)} %get-tuple-element.32.q_ref.k_ref.v_ref, ...), custom_call_target="tpu_custom_call" | custom-call | tf_op jit(solution)/shard_map/closing/pallas_call | solution.py:1225
  169.4 5.1 %finish.1 = (f32[4,1024]{1,0:T(4,128)}, f32[4,1024]{1,0:T(4,128)}, f32[4,1024]{1,0:T(4,128)}, f32[4,1024]{1,0:T(4,128)}, f32[2]{0:T(128)}, /*index=5*/bf16[4,256,1024]{2,1,0:T(8,128)(2,1)}, bf16[4,256,1024]{2,1,0:T(8,128)(2,1)}) custom-call(f32[24,1024]{1,0:T(8,128)} %get-tuple-element.47.total_ref, bf16[4,256,1024]{2,1,0:T(8,128)(2,1)} %get-tuple-element.48.a_hbm, ...), custom_call_target="tpu_custom_call" | custom-call | tf_op jit(solution)/shard_map/finish/pallas_call | solution.py:1301

commit v5 on v4

--- a/solution.py
+++ b/solution.py
@@ -1067,7 +1067,7 @@
             both = loc[a, near_rows, :] + near_sc[a, :, cols]
             grads[a, near_rows, cols] = (both * scales[a]).astype(bf16)
 
-    held = tile // 4
+    held = tile // 2
 
     def give(k):
         return remote(res_sc.at[peers[k][1]], out_ref.at[me], send.at[k], recv.at[k], peers[k])

time: 175 us -> 176 us (level)
  no operation moved by 1% of the time
where the time goes in v5:
time: 176 us
  Pallas kernels  175 us (99%)
    pallas_call x1, Pallas kernels, closing(): pl.pallas_call(functools.partial(close_kernel, size=size, strip=32, sizes...  64.4 us
    pallas_call x1, Pallas kernels, feed(): pl.pallas_call(functools.partial(feed_kernel, step=step), grid=(2,), in_s...  54.7 us
    pallas_call x1, Pallas kernels, opening(): pl.pallas_call(functools.partial(open_kernel, size=size, strip=32), grid=...  50.7 us
    pallas_call x1, Pallas kernels, finish(): pl.pallas_call(finish_kernel, in_specs=[VMEM, ANY, ANY], out_specs=[VMEM]...  5.14 us

profile of v5, /device:TPU:0, one launch (start us, length us, event | category | flops | bytes accessed | tf_op | source)
XLA Modules:
  0.0 175.8 jit_solution(13250792231926541314)
XLA Ops:
  0.6 50.7 %opening.1 = (bf16[4,256,1024]{2,1,0:T(8,128)(2,1)}, bf16[4,256,1024]{2,1,0:T(8,128)(2,1)}, f32[4,8,256]{2,1,0:T(8,128)}, bf16[1024,1024]{1,0:T(8,128)(2,1)}, bf...) custom-call(bf16[4,256,1024]{2,1,0:T(8,128)(2,1)} %x_ref.1, ...), custom_call_target="tpu_custom_call" | custom-call | tf_op jit(solution)/shard_map/opening/pallas_call | solution.py:679
  51.3 54.7 %feed.1 = (bf16[4,256,1024]{2,1,0:T(8,128)(2,1)}, bf16[4,256,1024]{2,1,0:T(8,128)(2,1)}, bf16[1024,1024]{1,0:T(8,128)(2,1)}, f32[8,1024]{1,0:T(8,128)}) custom-call(bf16[4,256,1024]{2,1,0:T(8,128)(2,1)} %get-tuple-element.33.x_hbm, bf16[4,256,1024]{2,1,0:T(8,128)(2,1)} %get-tuple-element.34.y_hbm, bf16[4,256,1024]{2,1,0:T(8,128)(2,1)} %dy_hbm.1, ...), custom_call_target="tpu_custom_call" | custom-call | tf_op jit(solution)/shard_map/feed/pallas_call | solution.py:906
  106.0 64.4 %closing.1 = (bf16[4,256,1024]{2,1,0:T(8,128)(2,1)}, bf16[4,256,1024]{2,1,0:T(8,128)(2,1)}, f32[24,1024]{1,0:T(8,128)}) custom-call(bf16[1024,3072]{1,0:T(8,128)(2,1)} %get-tuple-element.32.q_ref.k_ref.v_ref, bf16[1024,3072]{1,0:T(8,128)(2,1)} %get-tuple-element.32.q_ref.k_ref.v_ref, bf16[1024,3072]{1,0:T(8,128)(2,1)} %get-tuple-element.32.q_ref.k_ref.v_ref, ...), custom_call_target="tpu_custom_call" | custom-call | tf_op jit(solution)/shard_map/closing/pallas_call | solution.py:1225
  170.5 5.1 %finish.1 = (f32[4,1024]{1,0:T(4,128)}, f32[4,1024]{1,0:T(4,128)}, f32[4,1024]{1,0:T(4,128)}, f32[4,1024]{1,0:T(4,128)}, f32[2]{0:T(128)}, /*index=5*/bf16[4,256,1024]{2,1,0:T(8,128)(2,1)}, bf16[4,256,1024]{2,1,0:T(8,128)(2,1)}) custom-call(f32[24,1024]{1,0:T(8,128)} %get-tuple-element.47.total_ref, bf16[4,256,1024]{2,1,0:T(8,128)(2,1)} %get-tuple-element.48.a_hbm, ...), custom_call_target="tpu_custom_call" | custom-call | tf_op jit(solution)/shard_map/finish/pallas_call | solution.py:1301
